TPU v7x, 32 devices: a whole 2x2x4 slice. The times are simulated.
32 devices in a mesh: seq: 16 (over z, x, core), head: 2 (over y).
Axes of the slice: x: 2, y: 2, z: 4, core: 2. Of those that a mesh axis runs over, the one named last changes fastest.
Arguments:
- doppler_input: bfloat16 [32, 256, 768], P('seq', None, 'head'), may hold values from -14 to 14
- range_saved_input: bfloat16 [32, 256, 768], P('seq', None, 'head'), may hold values from -14 to 14
- layer_cot: bfloat16 [32, 256, 768], P('seq', None, 'head'), may hold values from -6 to 6
- qkv_doppler: bfloat16 [768, 2304], P(None, 'head'), may hold values from -1 to 1
- out_doppler: bfloat16 [768, 768], P('head'), may hold values from -0.21875 to 0.21875
- qkv_range: bfloat16 [768, 2304], P(None, 'head'), may hold values from -1 to 1
- out_range: bfloat16 [768, 768], P('head'), may hold values from -0.21875 to 0.21875
Outputs:
- input_grad: bfloat16 [32, 256, 768], P('seq', None, 'head')
- qkv_doppler_grad: float32 [768, 2304], P('seq', 'head')
- out_doppler_grad: float32 [768, 768], P('head', 'seq')
- qkv_range_grad: float32 [768, 2304], P('seq', 'head')
- out_range_grad: float32 [768, 768], P('head', 'seq')
All inputs are finite; a program needn't handle non-finite values.
Results may differ from a plain program's by a relative error of at most 0.014.
The roundings to bfloat16 on the way count: a program that leaves them out, or rounds other values in their place, can miss the bound.
Values may be sent and summed in bfloat16 or wider, within the bound.
A program may use at most 128 MiB of HBM per device.

v0:
```python
import jax
import jax.numpy as jnp
from jax import lax
from jax.sharding import PartitionSpec as P

HD = 64


DOPPLER_SHAPES = ("asu,avu->asv", "ojs,ost->ojt", "aru,ary->auy")
RANGE_SHAPES = ("mpw,cpw->pmc", "fdv,vfo->dfo", "nhr,hnp->rnp")
LEAD_CONTRACT = (((0,), (0,)), ((), ()))
TAIL_CONTRACT = (((1,), (1,)), ((), ()))


def swapped(block, axis, stride):
    count = lax.axis_size(axis)
    route = []
    for low in range(count):
        high = low | 1 << stride
        if high != low and high < count:
            route += [(low, high), (high, low)]
    return lax.ppermute(block, axis, route)


def head_backward(query, keys, values, grad_attn, forms, scale):
    scores = jnp.einsum(forms[0], query, keys, preferred_element_type=jnp.float32) * scale
    scores = scores - jnp.max(scores, axis=-1, keepdims=True)
    expo = jnp.exp(scores)
    probs = expo / jnp.sum(expo, axis=-1, keepdims=True)
    probs_low = probs.astype(jnp.bfloat16)
    attended = jnp.einsum(forms[1], probs_low, values, preferred_element_type=jnp.float32).astype(
        jnp.bfloat16
    )
    grad_values = jnp.einsum(
        forms[2], probs_low, grad_attn, preferred_element_type=jnp.float32
    ).astype(jnp.bfloat16)
    grad_probs = jnp.einsum(forms[0], grad_attn, values, preferred_element_type=jnp.float32)
    grad_scores = (
        probs * (grad_probs - jnp.sum(probs * grad_probs, axis=-1, keepdims=True)) * scale
    ).astype(jnp.bfloat16)
    grad_query = jnp.einsum(forms[1], grad_scores, keys, preferred_element_type=jnp.float32).astype(
        jnp.bfloat16
    )
    grad_keys = jnp.einsum(forms[2], grad_scores, query, preferred_element_type=jnp.float32).astype(
        jnp.bfloat16
    )
    return (attended, grad_query, grad_keys, grad_values)


def sublayer_local(inputs, cotangent, weight_qkv, weight_out, forms):
    width = inputs.shape[-1]
    leading = inputs.shape[:-1]
    flat_in = inputs.reshape(-1, width)
    flat_cot = cotangent.reshape(-1, width)
    heads_here = weight_out.shape[0] // HD
    projection = jnp.dot(flat_in, weight_qkv, preferred_element_type=jnp.float32).astype(
        jnp.bfloat16
    )
    projection = projection.reshape(leading + (heads_here, 3, HD))
    grad_attn = lax.dot_general(
        flat_cot, weight_out, TAIL_CONTRACT, preferred_element_type=jnp.float32
    )
    grad_attn = grad_attn.astype(jnp.bfloat16).reshape(leading + (heads_here, HD))
    scale = HD ** (-0.5)
    attended_list = []
    grad_list = []
    for head_index in range(heads_here):
        attended, grad_query, grad_keys, grad_values = head_backward(
            projection[..., head_index, 0, :],
            projection[..., head_index, 1, :],
            projection[..., head_index, 2, :],
            grad_attn[..., head_index, :],
            forms,
            scale,
        )
        attended_list.append(attended)
        grad_list.append(jnp.stack([grad_query, grad_keys, grad_values], axis=-2))
    attended = jnp.stack(attended_list, axis=-2).reshape(-1, heads_here * HD)
    grad_proj = jnp.stack(grad_list, axis=-3).reshape(-1, 3 * heads_here * HD)
    out_term = lax.dot_general(
        attended, flat_cot, LEAD_CONTRACT, preferred_element_type=jnp.float32
    )
    qkv_term = lax.dot_general(
        flat_in, grad_proj, LEAD_CONTRACT, preferred_element_type=jnp.float32
    )
    group_part = lax.dot_general(
        grad_proj, weight_qkv, TAIL_CONTRACT, preferred_element_type=jnp.float32
    )
    return (group_part.astype(jnp.bfloat16).reshape(inputs.shape), qkv_term, out_term)


def pair_weights(weight_qkv, weight_out, lower_half):
    other_qkv = swapped(weight_qkv, "head", 0)
    other_out = swapped(weight_out, "head", 0)
    full_qkv = jnp.where(
        lower_half,
        jnp.concatenate([weight_qkv, other_qkv], 1),
        jnp.concatenate([other_qkv, weight_qkv], 1),
    )
    full_out = jnp.where(
        lower_half,
        jnp.concatenate([weight_out, other_out], 0),
        jnp.concatenate([other_out, weight_out], 0),
    )
    return (full_qkv, full_out)


def reduction_terms(qkv_term, out_term, lower_half):
    half_width = qkv_term.shape[1] // 2
    half_rows = out_term.shape[0] // 2
    qkv_low, qkv_high = (qkv_term[:, :half_width], qkv_term[:, half_width:])
    out_low, out_high = (out_term[:half_rows], out_term[half_rows:])
    qkv_keep = jnp.where(lower_half, qkv_low, qkv_high)
    qkv_send = jnp.where(lower_half, qkv_high, qkv_low)
    out_keep = jnp.where(lower_half, out_low, out_high)
    out_send = jnp.where(lower_half, out_high, out_low)
    qkv_term = qkv_keep + swapped(qkv_send.astype(jnp.bfloat16), "head", 0).astype(qkv_send.dtype)
    out_term = out_keep + swapped(out_send.astype(jnp.bfloat16), "head", 0).astype(out_send.dtype)
    return (
        lax.psum_scatter(qkv_term, "seq", scatter_dimension=0, tiled=True),
        lax.psum_scatter(out_term, "seq", scatter_dimension=1, tiled=True),
    )


def shards(
    doppler_input, range_saved_input, layer_cot, qkv_doppler, out_doppler, qkv_range, out_range
):
    head_count = lax.axis_size("head")
    group_count = head_count // 2
    split_count = head_count // group_count
    position = lax.axis_index("head") % split_count
    lower_half = position == 0
    range_qkv, range_out = pair_weights(qkv_range, out_range, lower_half)
    doppler_qkv, doppler_out = pair_weights(qkv_doppler, out_doppler, lower_half)
    full_mid, full_cot = (
        lax.all_gather(range_saved_input, "head", axis=2, tiled=True),
        lax.all_gather(layer_cot, "head", axis=2, tiled=True),
    )
    column_middle, column_cot = (
        lax.all_to_all(full_mid, "seq", split_axis=1, concat_axis=0, tiled=True),
        lax.all_to_all(full_cot, "seq", split_axis=1, concat_axis=0, tiled=True),
    )
    part_width = column_middle.shape[1] // split_count
    column_start = position * part_width
    local_mid = lax.dynamic_slice_in_dim(column_middle, column_start, part_width, 1)
    local_cot = lax.dynamic_slice_in_dim(column_cot, column_start, part_width, 1)
    range_part, qkv_term, out_term = sublayer_local(
        local_mid, local_cot, range_qkv, range_out, RANGE_SHAPES
    )
    qkv_range_grad, out_range_grad = reduction_terms(qkv_term, out_term, lower_half)
    column_moved = lax.all_to_all(range_part, "head", split_axis=2, concat_axis=1, tiled=True)
    column_moved = column_moved.reshape(
        column_moved.shape[0], group_count, -1, column_moved.shape[2]
    )
    range_back = jnp.sum(column_moved, axis=1, dtype=jnp.float32).astype(jnp.bfloat16)
    row_backward_result = lax.all_to_all(range_back, "seq", split_axis=0, concat_axis=1, tiled=True)
    cotangent_mid = (
        layer_cot.astype(jnp.float32) + row_backward_result.astype(jnp.float32)
    ).astype(jnp.bfloat16)
    full_in, full_cot_mid = (
        lax.all_gather(doppler_input, "head", axis=2, tiled=True),
        lax.all_gather(cotangent_mid, "head", axis=2, tiled=True),
    )
    part_rows = full_in.shape[0] // split_count
    row_start = position * part_rows
    local_in = lax.dynamic_slice_in_dim(full_in, row_start, part_rows, 0)
    local_cot_mid = lax.dynamic_slice_in_dim(full_cot_mid, row_start, part_rows, 0)
    doppler_part, qkv_term, out_term = sublayer_local(
        local_in, local_cot_mid, doppler_qkv, doppler_out, DOPPLER_SHAPES
    )
    qkv_doppler_grad, out_doppler_grad = reduction_terms(qkv_term, out_term, lower_half)
    row_moved = lax.all_to_all(doppler_part, "head", split_axis=2, concat_axis=0, tiled=True)
    row_moved = row_moved.reshape(group_count, -1, row_moved.shape[1], row_moved.shape[2])
    doppler_back = jnp.sum(row_moved, axis=0, dtype=jnp.float32)
    input_grad = (cotangent_mid.astype(jnp.float32) + doppler_back).astype(jnp.bfloat16)
    return (input_grad, qkv_doppler_grad, out_doppler_grad, qkv_range_grad, out_range_grad)


def solution(mesh):
    placed = (
        P("seq", None, "head"),
        P("seq", None, "head"),
        P("seq", None, "head"),
        P(None, "head"),
        P("head", None),
        P(None, "head"),
        P("head", None),
    )
    return jax.shard_map(
        shards,
        mesh=mesh,
        in_specs=placed,
        out_specs=(
            P("seq", None, "head"),
            P("seq", "head"),
            P("head", "seq"),
            P("seq", "head"),
            P("head", "seq"),
        ),
        check_vma=False,
    )
```

profile of v0, /device:TPU:0, one launch (start us, length us, event | category | flops | bytes accessed | tf_op | source)
XLA Modules:
  0.0 609.9 jit_solution(12095630955462556774)
XLA Ops:
  8.6 13.0 %all_gather.12 = bf16[2,256,768]{2,0,1:T(2,128)(2,1)} all-gather(bf16[2,256,384]{2,0,1:T(2,128)(2,1)S(1)} %copy.426), channel_id=1, replica_groups=mesh['seq'=16,'head'=2] {'head'}, dimensions={2}, use_global_device_ids=true | all-gather | bytes 1179648 | tf_op jit(solution)/shard_map/all_gather | solution.py:136
  21.6 6.2 %all-to-all-start = ((bf16[2,256,768]{2,0,1:T(2,128)(2,1)}), bf16[2,256,768]{2,0,1:T(2,128)(2,1)S(1)}, u32[]{:S(2)}, u32[]{:S(2)}) async-start(bf16[2,256,768]{2,0,1:T(2,128)(2,1)} %all_gather.12), calls=%async_computation | async-start | bytes 1572864 | tf_op jit(solution)/shard_map/all_to_all | solution.py:140
  28.2 12.4 %all_gather.13 = bf16[2,256,768]{2,0,1:T(2,128)(2,1)} all-gather(bf16[2,256,384]{2,0,1:T(2,128)(2,1)S(1)} %copy.431), channel_id=1, replica_groups=mesh['seq'=16,'head'=2] {'head'}, dimensions={2}, use_global_device_ids=true | all-gather | bytes 1179648 | tf_op jit(solution)/shard_map/all_gather | solution.py:137
  40.5 5.9 all-to-all-done
  46.4 5.5 all-to-all-start.1
  56.0 108.7 %all_gather.14 = bf16[2,256,768]{2,1,0:T(8,128)(2,1)} all-gather(bf16[2,256,384]{2,1,0:T(8,128)(2,1)S(1)} %copy-done.35), channel_id=1, replica_groups=mesh['seq'=16,'head'=2] {'head'}, dimensions={2}, use_global_device_ids=true | all-gather | bytes 1179648 | tf_op jit(solution)/shard_map/all_gather | solution.py:161
  169.6 4.2 convolution_convert_fusion.1
  173.8 5.9 reshape.965
  259.3 3.7 copy.492
  263.0 6.3 %reshape.968 = bf16[256,2304]{1,0:T(8,128)(2,1)} reshape(bf16[32,8,12,3,64]{4,3,2,1,0:T(4,128)(2,1)} %copy.492) | data formatting | bytes 2359296 | tf_op jit(solution)/shard_map/reshape | solution.py:79
  277.7 4.0 fusion.24
  284.7 3.8 reshape.1035
  288.5 4.2 all-to-all-start.2
  303.8 16.8 %all-to-all-done.2 = bf16[2,2,49152]{2,1,0:T(2,128)(2,1)} async-done(((bf16[2,2,49152]{2,1,0:T(2,128)(2,1)}), bf16[2,2,49152]{2,1,0:T(2,128)(2,1)}, u32[]{:S(2)}, u32[]{:S(2)}) %all-to-all-start.2) | async-done | bytes 393248 | tf_op jit(solution)/shard_map/all_to_all | solution.py:151
  326.3 5.6 all-to-all-start.3
  340.4 3.7 all-to-all-done.3
  345.4 11.8 %all_gather.15 = bf16[2,256,768]{2,1,0:T(8,128)(2,1)S(1)} all-gather(bf16[2,256,384]{2,1,0:T(8,128)(2,1)S(1)} %fusion.231), channel_id=1, replica_groups=mesh['seq'=16,'head'=2] {'head'}, dimensions={2}, use_global_device_ids=true | all-gather | bytes 1179648 | tf_op jit(solution)/shard_map/all_gather | solution.py:162
  376.1 11.2 %collective-permute-done.5 = bf16[384,768]{1,0:T(8,128)(2,1)S(1)} collective-permute-done((bf16[384,768]{1,0:T(8,128)(2,1)S(1)}, bf16[384,768]{1,0:T(8,128)(2,1)S(1)}, u32[]{:S(2)}, u32[]{:S(2)}) %collective-permute-start.5) | collective-permute-done | bytes 589856 | tf_op jit(solution)/shard_map/ppermute | solution.py:22
  392.7 6.0 convert_add_fusion
  404.8 38.3 %collective-permute-done.4 = bf16[768,1152]{1,0:T(8,128)(2,1)S(1)} collective-permute-done((bf16[768,1152]{1,0:T(8,128)(2,1)S(1)}, bf16[768,1152]{1,0:T(8,128)(2,1)S(1)}, u32[]{:S(2)}, u32[]{:S(2)}) %collective-permute-start.4) | collective-permute-done | bytes 1769504 | tf_op jit(solution)/shard_map/ppermute | solution.py:22
  445.3 4.3 fusion.25
  453.9 8.3 %all_to_all.69 = bf16[2,2,49152]{2,1,0:T(2,128)(2,1)S(1)} all-to-all(bf16[2,2,49152]{2,1,0:T(2,128)(2,1)S(1)} %reshape.1037), channel_id=1, replica_groups=mesh['seq'=16,'head'=2] {'head'}, dimensions={0} | all-to-all | bytes 786432 | tf_op jit(solution)/shard_map/all_to_all | solution.py:172
  463.6 68.2 %reduce-scatter.11.cloned.1.call-done = f32[48,1152]{1,0:T(8,128)} async-done(((f32[768,1152]{1,0:T(8,128)}), f32[48,1152]{1,0:T(8,128)}) %reduce-scatter.11.cloned.1.call-update) | async-done | bytes 221200 | tf_op jit(solution)/shard_map/reduce_scatter | solution.py:120
  531.9 71.3 %reduce-scatter.9.cloned.1.call-done = f32[48,1152]{1,0:T(8,128)} async-done(((f32[768,1152]{1,0:T(8,128)}), f32[48,1152]{1,0:T(8,128)}) %reduce-scatter.9.cloned.1.call-update) | async-done | bytes 221200 | tf_op jit(solution)/shard_map/reduce_scatter | solution.py:120
  (717 shorter events, 164.0 us)
Async XLA Ops:
  21.6 24.9 %all-to-all-start = ((bf16[2,256,768]{2,0,1:T(2,128)(2,1)}), bf16[2,256,768]{2,0,1:T(2,128)(2,1)S(1)}, u32[]{:S(2)}, u32[]{:S(2)}) async-start(bf16[2,256,768]{2,0,1:T(2,128)(2,1)} %all_gather.12), calls=%async_computation | async-start | bytes 1572864 | tf_op jit(solution)/shard_map/all_to_all | solution.py:140
  28.1 25.4 %copy-start.172 = (bf16[384,768]{1,0:T(8,128)(2,1)S(1)}, bf16[384,768]{1,0:T(8,128)(2,1)}, u32[]{:S(2)}) copy-start(bf16[384,768]{1,0:T(8,128)(2,1)} %param.13) | copy-start | bytes 1769476
  28.2 27.9 %copy-start.35 = (bf16[2,256,384]{2,1,0:T(8,128)(2,1)S(1)}, bf16[2,256,384]{2,1,0:T(8,128)(2,1)}, u32[]{:S(2)}) copy-start(bf16[2,256,384]{2,1,0:T(8,128)(2,1)} %param.7) | copy-start | bytes 1179652
  46.4 118.5 %all-to-all-start.1 = ((bf16[2,256,768]{2,0,1:T(2,128)(2,1)}), bf16[2,256,768]{2,0,1:T(2,128)(2,1)S(1)}, u32[]{:S(2)}, u32[]{:S(2)}) async-start(bf16[2,256,768]{2,0,1:T(2,128)(2,1)} %all_gather.13), calls=%async_computation.1 | async-start | bytes 1572864 | tf_op jit(solution)/shard_map/all_to_all | solution.py:141
  51.9 117.7 %collective-permute-start = (bf16[768,1152]{1,0:T(8,128)(2,1)}, bf16[768,1152]{1,0:T(8,128)(2,1)}, u32[]{:S(2)}, u32[]{:S(2)}) collective-permute-start(bf16[768,1152]{1,0:T(8,128)(2,1)} %param.12), channel_id=1, source_target_pairs={{0,1},{1,0},{2,3},{3,2},{4,5},{5,4},{6,7},{7,6},{8,9},{9,8},{10,11... | collective-permute-start | bytes 5308424 | tf_op jit(solution)/shard_map/ppermute | solution.py:22
  53.5 111.7 %collective-permute-start.1 = (bf16[384,768]{1,0:T(8,128)(2,1)S(1)}, bf16[384,768]{1,0:T(8,128)(2,1)S(1)}, u32[]{:S(2)}, u32[]{:S(2)}) collective-permute-start(bf16[384,768]{1,0:T(8,128)(2,1)S(1)} %copy-done.172), channel_id=1, source_target_pairs={{0,1},{1,0},{2,3},{3,2},{4,5},{5,4},{6,7},{7,6},{8,9},{9,8},{10,11... | collective-permute-start | bytes 1769480 | tf_op jit(solution)/shard_map/ppermute | solution.py:22
  54.0 174.6 %collective-permute-start.2 = (bf16[768,1152]{1,0:T(8,128)(2,1)}, bf16[768,1152]{1,0:T(8,128)(2,1)}, u32[]{:S(2)}, u32[]{:S(2)}) collective-permute-start(bf16[768,1152]{1,0:T(8,128)(2,1)} %param.10), channel_id=1, source_target_pairs={{0,1},{1,0},{2,3},{3,2},{4,5},{5,4},{6,7},{7,6},{8,9},{9,8},{10,11... | collective-permute-start | bytes 5308424 | tf_op jit(solution)/shard_map/ppermute | solution.py:22
  55.5 301.6 %collective-permute-start.3 = (bf16[384,768]{1,0:T(8,128)(2,1)}, bf16[384,768]{1,0:T(8,128)(2,1)}, u32[]{:S(2)}, u32[]{:S(2)}) collective-permute-start(bf16[384,768]{1,0:T(8,128)(2,1)} %param.11), channel_id=1, source_target_pairs={{0,1},{1,0},{2,3},{3,2},{4,5},{5,4},{6,7},{7,6},{8,9},{9,8},{10,11... | collective-permute-start | bytes 1769480 | tf_op jit(solution)/shard_map/ppermute | solution.py:22
  192.5 26.2 %copy-start.175 = (f32[8,32,32]{1,2,0:T(8,128)}, f32[8,32,32]{1,2,0:T(8,128)S(1)}, u32[]{:S(2)}) copy-start(f32[8,32,32]{1,2,0:T(8,128)S(1)} %get-tuple-element.104) | copy-start | bytes 98308
  192.5 26.2 %copy-start.201 = (f32[8,32]{1,0:T(8,128)}, f32[8,32]{1,0:T(8,128)S(1)}, u32[]{:S(2)}) copy-start(f32[8,32]{1,0:T(8,128)S(1)} %get-tuple-element.103) | copy-start | bytes 3076
  194.6 24.9 %copy-start.177 = (f32[8,32,32]{1,2,0:T(8,128)}, f32[8,32,32]{1,2,0:T(8,128)S(1)}, u32[]{:S(2)}) copy-start(f32[8,32,32]{1,2,0:T(8,128)S(1)} %get-tuple-element.102) | copy-start | bytes 98308
  194.6 24.9 %copy-start.203 = (f32[8,32]{1,0:T(8,128)}, f32[8,32]{1,0:T(8,128)S(1)}, u32[]{:S(2)}) copy-start(f32[8,32]{1,0:T(8,128)S(1)} %get-tuple-element.101) | copy-start | bytes 3076
  196.7 23.6 %copy-start.179 = (f32[8,32,32]{1,2,0:T(8,128)}, f32[8,32,32]{1,2,0:T(8,128)S(1)}, u32[]{:S(2)}) copy-start(f32[8,32,32]{1,2,0:T(8,128)S(1)} %get-tuple-element.100) | copy-start | bytes 98308
  196.7 23.6 %copy-start.205 = (f32[8,32]{1,0:T(8,128)}, f32[8,32]{1,0:T(8,128)S(1)}, u32[]{:S(2)}) copy-start(f32[8,32]{1,0:T(8,128)S(1)} %get-tuple-element.99) | copy-start | bytes 3076
  256.1 79.3 %collective-permute-start.7 = (bf16[384,768]{1,0:T(8,128)(2,1)}, bf16[384,768]{1,0:T(8,128)(2,1)}, u32[]{:S(2)}, u32[]{:S(2)}) collective-permute-start(bf16[384,768]{1,0:T(8,128)(2,1)} %select_convert_fusion.2), channel_id=1, source_target_pairs={{0,1},{1,0},{2,3},{3,2},{4,5},{5,4},{6,7},{7,6},{8,9},{9,8},{10,11... | collective-permute-start | bytes 1769480 | tf_op jit(solution)/shard_map/ppermute | solution.py:22
  276.3 116.4 %collective-permute-start.6 = (bf16[768,1152]{1,0:T(8,128)(2,1)}, bf16[768,1152]{1,0:T(8,128)(2,1)}, u32[]{:S(2)}, u32[]{:S(2)}) collective-permute-start(bf16[768,1152]{1,0:T(8,128)(2,1)} %select_convert_fusion), channel_id=1, source_target_pairs={{0,1},{1,0},{2,3},{3,2},{4,5},{5,4},{6,7},{7,6},{8,9},{9,8},{10,11... | collective-permute-start | bytes 5308424 | tf_op jit(solution)/shard_map/ppermute | solution.py:22
  288.5 32.1 %all-to-all-start.2 = ((bf16[2,2,49152]{2,1,0:T(2,128)(2,1)}), bf16[2,2,49152]{2,1,0:T(2,128)(2,1)}, u32[]{:S(2)}, u32[]{:S(2)}) async-start(bf16[2,2,49152]{2,1,0:T(2,128)(2,1)} %reshape.1035), calls=%async_computation.2 | async-start | bytes 786432 | tf_op jit(solution)/shard_map/all_to_all | solution.py:151
  326.3 17.8 %all-to-all-start.3 = ((bf16[32,16,384]{2,1,0:T(8,128)(2,1)}), bf16[32,16,384]{2,1,0:T(8,128)(2,1)}, u32[]{:S(2)}, u32[]{:S(2)}) async-start(bf16[32,16,384]{2,1,0:T(8,128)(2,1)} %bitcast.1223), calls=%async_computation.3 | async-start | bytes 786432 | tf_op jit(solution)/shard_map/all_to_all | solution.py:156
  331.8 131.8 %reduce-scatter.15.cloned.1.call-start = ((), (), s32[]{:S(2)}) async-start(), calls=%async_computation.12 | async-start | bytes 1253376
  340.3 123.3 %reduce-scatter.13.cloned.1.call-start = ((), (), s32[]{:S(2)}) async-start(), calls=%async_computation.11 | async-start | bytes 1253376
  372.8 14.6 %collective-permute-start.5 = (bf16[384,768]{1,0:T(8,128)(2,1)S(1)}, bf16[384,768]{1,0:T(8,128)(2,1)S(1)}, u32[]{:S(2)}, u32[]{:S(2)}) collective-permute-start(bf16[384,768]{1,0:T(8,128)(2,1)S(1)} %select_convert_fusion.3), channel_id=1, source_target_pairs={{0,1},{1,0},{2,3},{3,2},{4,5},{5,4},{6,7},{7,6},{8,9},{9,8},{10,11... | collective-permute-start | bytes 1769480 | tf_op jit(solution)/shard_map/ppermute | solution.py:22
  389.0 142.9 %reduce-scatter.11.cloned.1.call-start = ((), (), s32[]{:S(2)}) async-start(), calls=%async_computation.10 | async-start | bytes 3760128 | tf_op jit(solution)/shard_map/reduce_scatter | solution.py:120
  398.7 204.5 %reduce-scatter.9.cloned.1.call-start = ((), (), s32[]{:S(2)}) async-start(), calls=%async_computation.9 | async-start | bytes 3760128 | tf_op jit(solution)/shard_map/reduce_scatter | solution.py:120
  404.2 38.9 %collective-permute-start.4 = (bf16[768,1152]{1,0:T(8,128)(2,1)S(1)}, bf16[768,1152]{1,0:T(8,128)(2,1)S(1)}, u32[]{:S(2)}, u32[]{:S(2)}) collective-permute-start(bf16[768,1152]{1,0:T(8,128)(2,1)S(1)} %select_convert_fusion.1), channel_id=1, source_target_pairs={{0,1},{1,0},{2,3},{3,2},{4,5},{5,4},{6,7},{7,6},{8,9},{9,8},{10,11... | collective-permute-start | bytes 5308424 | tf_op jit(solution)/shard_map/ppermute | solution.py:22
  (220 other events, 591.4 us)
Sparse Core Ops, SparseCore 0:
  340.5 58.5 reduce-scatter.14
  403.2 57.0 reduce-scatter.12
  464.8 67.0 reduce-scatter.10
  536.2 66.9 reduce-scatter.8
where the time goes:
time: 617 us; the launch traced here: 610 us
  waiting for transfers between devices  216 us (35%)
  blocking collectives  154 us (25%)
  matrix products  112 us (18%)
  local copies, waits for them, and re-layouts  58.4 us (9%)
  starting transfers between devices  29.1 us (5%)
  other arithmetic  23.3 us (4%)
  between operations  16.8 us (3%)
    reduce_scatter x2, waiting for transfers between devices, reduction_terms(): lax.psum_scatter(qkv_term, 'seq', scatter_dimension=0, tiled=True)  140 us
    all_gather x1, blocking collectives, shards(): lax.all_gather(doppler_input, 'head', axis=2, tiled=True)  109 us
    ppermute x8, waiting for transfers between devices, swapped(): return lax.ppermute(block, axis, route)  49.6 us
    unnamed x465, local copies, waits for them, and re-layouts  23 us
    all_to_all x1, waiting for transfers between devices, shards(): lax.all_to_all(range_part, 'head', split_axis=2, concat_axis=1, tiled=True)  16.8 us
    dot_general x12, matrix products, head_backward(): jnp.einsum(forms[0], query, keys, preferred_element_type=jnp.float32)  15.8 us
    dot_general x24, matrix products, head_backward(): jnp.einsum(forms[1], probs_low, values, preferred_element_type=jnp.float32)  15.8 us
    dot_general x24, matrix products, head_backward(): jnp.einsum(forms[1], grad_scores, keys, preferred_element_type=jnp.float32)  14.8 us
  transfers between devices with their start and end apart: 16, of which 7 were waited for; matrix products, arithmetic and copies ran while one was open for 30% of the time, Pallas kernels for 0%

commit v1 on v0

--- a/solution.py
+++ b/solution.py
@@ -176,6 +176,95 @@
     return (input_grad, qkv_doppler_grad, out_doppler_grad, qkv_range_grad, out_range_grad)
 
 
+def both_halves(mine, other, lower_half):
+    return jnp.where(
+        lower_half, jnp.concatenate([mine, other], -1), jnp.concatenate([other, mine], -1)
+    )
+
+
+def heads_sublayer(inputs, cotangent, weight_qkv, weight_out, forms, lower_half):
+    width = inputs.shape[-1]
+    leading = inputs.shape[:-1]
+    flat_in = inputs.reshape(-1, width)
+    flat_cot = cotangent.reshape(-1, width)
+    heads_here = weight_out.shape[0] // HD
+    projection = jnp.dot(flat_in, weight_qkv, preferred_element_type=jnp.float32).astype(
+        jnp.bfloat16
+    )
+    projection = projection.reshape(leading + (heads_here, 3, HD))
+    grad_attn = lax.dot_general(
+        flat_cot, weight_out, TAIL_CONTRACT, preferred_element_type=jnp.float32
+    )
+    grad_attn = grad_attn.astype(jnp.bfloat16).reshape(leading + (heads_here, HD))
+    scale = HD ** (-0.5)
+    attended_list = []
+    grad_list = []
+    for head_index in range(heads_here):
+        attended, grad_query, grad_keys, grad_values = head_backward(
+            projection[..., head_index, 0, :],
+            projection[..., head_index, 1, :],
+            projection[..., head_index, 2, :],
+            grad_attn[..., head_index, :],
+            forms,
+            scale,
+        )
+        attended_list.append(attended)
+        grad_list += [grad_query, grad_keys, grad_values]
+    attended = jnp.concatenate(attended_list, axis=-1).reshape(-1, heads_here * HD)
+    grad_proj = jnp.concatenate(grad_list, axis=-1).reshape(-1, 3 * heads_here * HD)
+    out_term = lax.dot_general(
+        flat_cot, attended, LEAD_CONTRACT, preferred_element_type=jnp.float32
+    )
+    qkv_term = lax.dot_general(
+        flat_in, grad_proj, LEAD_CONTRACT, preferred_element_type=jnp.float32
+    )
+    part = lax.dot_general(
+        grad_proj, weight_qkv, TAIL_CONTRACT, preferred_element_type=jnp.float32
+    )
+    half = width // 2
+    keep = jnp.where(lower_half, part[:, :half], part[:, half:])
+    send = jnp.where(lower_half, part[:, half:], part[:, :half])
+    part = keep + swapped(send.astype(jnp.bfloat16), "head", 0).astype(jnp.float32)
+    return (part.reshape(leading + (half,)), qkv_term, out_term)
+
+
+def scattered_sum(term):
+    count = lax.axis_size("seq")
+    pieces = term.astype(jnp.bfloat16).reshape((count, -1) + term.shape[1:])
+    pieces = lax.all_to_all(pieces, "seq", split_axis=0, concat_axis=0, tiled=True)
+    return jnp.sum(pieces.astype(jnp.float32), axis=0)
+
+
+def shards_by_head(
+    doppler_input, range_saved_input, layer_cot, qkv_doppler, out_doppler, qkv_range, out_range
+):
+    lower_half = lax.axis_index("head") == 0
+    both = jnp.stack([range_saved_input, layer_cot])
+    both = lax.all_to_all(both, "seq", split_axis=2, concat_axis=1, tiled=True)
+    both = both_halves(both, swapped(both, "head", 0), lower_half)
+    part, qkv_term, out_term = heads_sublayer(
+        both[0], both[1], qkv_range, out_range, RANGE_SHAPES, lower_half
+    )
+    range_back = part.astype(jnp.bfloat16)
+    range_back = lax.all_to_all(range_back, "seq", split_axis=0, concat_axis=1, tiled=True)
+    cotangent_mid = (layer_cot.astype(jnp.float32) + range_back.astype(jnp.float32)).astype(
+        jnp.bfloat16
+    )
+    qkv_range_grad = scattered_sum(qkv_term)
+    out_range_grad = scattered_sum(out_term).T
+    full_in = both_halves(doppler_input, swapped(doppler_input, "head", 0), lower_half)
+    full_cot = both_halves(cotangent_mid, swapped(cotangent_mid, "head", 0), lower_half)
+    part, qkv_term, out_term = heads_sublayer(
+        full_in, full_cot, qkv_doppler, out_doppler, DOPPLER_SHAPES, lower_half
+    )
+    input_grad = (
+        cotangent_mid.astype(jnp.float32) + part.astype(jnp.bfloat16).astype(jnp.float32)
+    ).astype(jnp.bfloat16)
+    qkv_doppler_grad = scattered_sum(qkv_term)
+    out_doppler_grad = scattered_sum(out_term).T
+    return (input_grad, qkv_doppler_grad, out_doppler_grad, qkv_range_grad, out_range_grad)
+
+
 def solution(mesh):
     placed = (
         P("seq", None, "head"),
@@ -187,7 +276,7 @@
         P("head", None),
     )
     return jax.shard_map(
-        shards,
+        shards_by_head if mesh.shape["head"] == 2 else shards,
         mesh=mesh,
         in_specs=placed,
         out_specs=(

time: 617 us -> 300 us (0.49)
  the two profiles are of different devices: /device:TPU:0 before, /device:TPU:11 now
where the time goes in v1:
time: 300 us; the launch traced here: 295 us
  matrix products  132 us (44%)
  waiting for transfers between devices  75 us (25%)
  starting transfers between devices  39 us (13%)
  local copies, waits for them, and re-layouts  38 us (13%)
  other arithmetic  9.09 us (3%)
    all_to_all x4, waiting for transfers between devices, scattered_sum(): lax.all_to_all(pieces, 'seq', split_axis=0, concat_axis=0, tiled=True)  45.8 us
    ppermute x5, waiting for transfers between devices, swapped(): return lax.ppermute(block, axis, route)  25 us
    dot_general x12, matrix products, head_backward(): jnp.einsum(forms[2], grad_scores, query, preferred_element_type=jnp.float32)  24.2 us
    dot_general x12, matrix products, head_backward(): jnp.einsum(forms[1], grad_scores, keys, preferred_element_type=jnp.float32)  23.9 us
    all_to_all x4, starting transfers between devices, scattered_sum(): lax.all_to_all(pieces, 'seq', split_axis=0, concat_axis=0, tiled=True)  21 us
    dot_general x12, matrix products, head_backward(): jnp.einsum(forms[2], probs_low, grad_attn, preferred_element_type=jnp.flo...  18.8 us
    sub x12, matrix products, head_backward(): scores = scores - jnp.max(scores, axis=-1, keepdims=True)  18.5 us
    dot_general x12, matrix products, head_backward(): jnp.einsum(forms[1], probs_low, values, preferred_element_type=jnp.float32)  17.9 us
  transfers between devices with their start and end apart: 11, of which 9 were waited for; matrix products, arithmetic and copies ran while one was open for 32% of the time, Pallas kernels for 0%

profile of v1, /device:TPU:11, one launch (start us, length us, event | category | flops | bytes accessed | tf_op | source)
XLA Modules:
  0.0 294.6 jit_solution(13812560884693935236)
XLA Ops:
  5.8 7.6 %all-to-all-start = ((bf16[2,2,256,384]{3,1,0,2:T(2,128)(2,1)}), bf16[2,2,256,384]{3,1,0,2:T(2,128)(2,1)}, u32[]{:S(2)}, u32[]{:S(2)}) async-start(bf16[2,2,256,384]{3,1,0,2:T(2,128)(2,1)} %pad_maximum_fusion), calls=%async_computation | async-start | bytes 1572864 | tf_op jit(solution)/shard_map/all_to_all | solution.py:243
  14.2 2.9 convolution_convert_fusion.1
  18.6 2.9 reshape.103
  43.2 10.5 %collective-permute-done = bf16[2,32,16,384]{3,2,1,0:T(8,128)(2,1)S(1)} collective-permute-done((bf16[2,32,16,384]{3,2,1,0:T(8,128)(2,1)S(1)}, bf16[2,32,16,384]{3,2,1,0:T(8,128)(2,1)S(1)}, u32[]{:S(2)}, u32[]{:S(2)}) %collective-permute-start) | collective-permute-done | bytes 786464 | tf_op jit(solution)/shard_map/ppermute | solution.py:22
  60.5 3.2 %reshape.100 = bf16[32,16,6,3,64]{4,3,2,1,0:T(4,128)(2,1)} reshape(bf16[512,1152]{1,0:T(8,128)(2,1)S(1)} %convolution_convert_fusion.2) | data formatting | bytes 2359296 | tf_op jit(solution)/shard_map/reshape | solution.py:194
  63.7 8.7 %fusion.356 = (bf16[32,16,1,1,64]{4,3,2,1,0:T(2,128)(2,1)}, bf16[32,16,1,1,64]{4,3,2,1,0:T(2,128)(2,1)}, bf16[32,16,1,1,64]{4,3,2,1,0:T(2,128)(2,1)S(1)}, bf16[3...) fusion(bf16[32,16,6,3,64]{4,3,2,1,0:T(4,128)(2,1)} %reshape.100), kind=kLoop, calls=%fused_computation.490 | loop fusion | bytes 2359296 | tf_op jit(solution)/shard_map/slice | solution.py:204
  122.9 2.9 concatenate.52
  132.0 5.1 %collective-permute-done.1 = bf16[512,384]{1,0:T(8,128)(2,1)S(1)} collective-permute-done((bf16[512,384]{1,0:T(8,128)(2,1)S(1)}, bf16[512,384]{1,0:T(8,128)(2,1)S(1)}, u32[]{:S(2)}, u32[]{:S(2)}) %collective-permute-start.1) | collective-permute-done | bytes 393248 | tf_op jit(solution)/shard_map/ppermute | solution.py:22
  137.9 7.9 %all-to-all-start.1 = ((bf16[32,16,384]{2,1,0:T(8,128)(2,1)}), bf16[32,16,384]{2,1,0:T(8,128)(2,1)S(1)}, u32[]{:S(2)}, u32[]{:S(2)}) async-start(bf16[32,16,384]{2,1,0:T(8,128)(2,1)} %bitcast.50), calls=%async_computation.1 | async-start | bytes 786432 | tf_op jit(solution)/shard_map/all_to_all | solution.py:249
  152.3 4.3 %all-to-all-done.1 = bf16[32,16,384]{2,1,0:T(8,128)(2,1)S(1)} async-done(((bf16[32,16,384]{2,1,0:T(8,128)(2,1)}), bf16[32,16,384]{2,1,0:T(8,128)(2,1)S(1)}, u32[]{:S(2)}, u32[]{:S(2)}) %all-to-all-start.1) | async-done | bytes 393248 | tf_op jit(solution)/shard_map/all_to_all | solution.py:249
  159.3 5.0 %all-to-all-start.5 = ((bf16[16,48,384]{2,1,0:T(8,128)(2,1)}), bf16[16,48,384]{2,1,0:T(8,128)(2,1)S(1)}, u32[]{:S(2)}, u32[]{:S(2)}) async-start(bf16[16,48,384]{2,1,0:T(8,128)(2,1)} %bitcast.97), calls=%async_computation.5 | async-start | bytes 1179648 | tf_op jit(solution)/shard_map/all_to_all | solution.py:234
  164.2 2.4 convolution_convert_fusion
  176.4 2.6 fusion.25
  179.2 5.7 %all-to-all-start.3 = ((bf16[16,48,384]{2,1,0:T(8,128)(2,1)}), bf16[16,48,384]{2,1,0:T(8,128)(2,1)S(1)}, u32[]{:S(2)}, u32[]{:S(2)}) async-start(bf16[16,48,384]{2,1,0:T(8,128)(2,1)} %bitcast.87), calls=%async_computation.3 | async-start | bytes 1179648 | tf_op jit(solution)/shard_map/all_to_all | solution.py:234
  192.8 7.1 %all-to-all-done.3 = bf16[16,48,384]{2,1,0:T(8,128)(2,1)S(1)} async-done(((bf16[16,48,384]{2,1,0:T(8,128)(2,1)}), bf16[16,48,384]{2,1,0:T(8,128)(2,1)S(1)}, u32[]{:S(2)}, u32[]{:S(2)}) %all-to-all-start.3) | async-done | bytes 589856 | tf_op jit(solution)/shard_map/all_to_all | solution.py:234
  200.8 5.3 %all-to-all-start.4 = ((bf16[16,48,1152]{2,1,0:T(8,128)(2,1)}), bf16[16,48,1152]{2,1,0:T(8,128)(2,1)S(1)}, u32[]{:S(2)}, u32[]{:S(2)}) async-start(bf16[16,48,1152]{2,1,0:T(8,128)(2,1)} %bitcast.641), calls=%async_computation.4 | async-start | bytes 3538944 | tf_op jit(solution)/shard_map/all_to_all | solution.py:234
  209.7 2.2 fusion.130
  226.9 3.7 %fusion.24 = bf16[768,1152]{1,0:T(8,128)(2,1)} fusion(bf16[2,256,1152]{1,2,0:T(8,128)(2,1)} %fusion.134, bf16[2,256,384]{2,1,0:T(8,128)(2,1)S(1)} %copy-done.90, bf16[2,256,384]{2,1,0:T(8,128)(2,1)S(1)} %copy-done.88, pred[]{:T(512)S(6)} %eq.3), kind=kOutput, calls=%fused_computation.27 | convolution fusion | flops 910393344 | bytes 3735553 | tf_op jit(solution)/shard_map/dot_general | solution.py:218
  230.6 15.8 %all-to-all-done.4 = bf16[16,48,1152]{2,1,0:T(8,128)(2,1)S(1)} async-done(((bf16[16,48,1152]{2,1,0:T(8,128)(2,1)}), bf16[16,48,1152]{2,1,0:T(8,128)(2,1)S(1)}, u32[]{:S(2)}, u32[]{:S(2)}) %all-to-all-start.4) | async-done | bytes 1769504 | tf_op jit(solution)/shard_map/all_to_all | solution.py:234
  246.4 5.0 %all-to-all-start.2 = ((bf16[16,48,1152]{2,1,0:T(8,128)(2,1)}), bf16[16,48,1152]{2,1,0:T(8,128)(2,1)}, u32[]{:S(2)}, u32[]{:S(2)}) async-start(bf16[16,48,1152]{2,1,0:T(8,128)(2,1)} %bitcast.85), calls=%async_computation.2 | async-start | bytes 3538944 | tf_op jit(solution)/shard_map/all_to_all | solution.py:234
  252.8 3.0 %fusion.374 = f32[512,768]{1,0:T(8,128)S(1)} fusion(bf16[512,1152]{1,0:T(8,128)(2,1)} %bitcast.647, bf16[768,1152]{1,0:T(8,128)(2,1)} %param.10), kind=kOutput, calls=%fused_computation.508 | convolution fusion | flops 905969664 | bytes 4521984 | tf_op jit(solution)/shard_map/dot_general | solution.py:221
  257.7 8.7 %collective-permute-done.4 = bf16[512,384]{1,0:T(8,128)(2,1)S(1)} collective-permute-done((bf16[512,384]{1,0:T(8,128)(2,1)S(1)}, bf16[512,384]{1,0:T(8,128)(2,1)S(1)}, u32[]{:S(2)}, u32[]{:S(2)}) %collective-permute-start.4) | collective-permute-done | bytes 393248 | tf_op jit(solution)/shard_map/ppermute | solution.py:22
  269.3 22.6 %all-to-all-done.2 = bf16[16,48,1152]{2,1,0:T(8,128)(2,1)} async-done(((bf16[16,48,1152]{2,1,0:T(8,128)(2,1)}), bf16[16,48,1152]{2,1,0:T(8,128)(2,1)}, u32[]{:S(2)}, u32[]{:S(2)}) %all-to-all-start.2) | async-done | bytes 1769504 | tf_op jit(solution)/shard_map/all_to_all | solution.py:234
  291.9 2.4 convert_reduce_fusion.1
  (306 shorter events, 145.1 us)
Async XLA Ops:
  0.6 58.6 %copy-start = (bf16[768,1152]{1,0:T(8,128)(2,1)S(1)}, bf16[768,1152]{1,0:T(8,128)(2,1)}, u32[]{:S(2)}) copy-start(bf16[768,1152]{1,0:T(8,128)(2,1)} %param.12) | copy-start | bytes 5308420
  0.6 12.8 %collective-permute-start.2 = (bf16[2,256,384]{2,1,0:T(8,128)(2,1)}, bf16[2,256,384]{2,1,0:T(8,128)(2,1)S(1)}, u32[]{:S(2)}, u32[]{:S(2)}) collective-permute-start(bf16[2,256,384]{2,1,0:T(8,128)(2,1)} %param.7), channel_id=1, source_target_pairs={{0,1},{1,0},{2,3},{3,2},{4,5},{5,4},{6,7},{7,6},{8,9},{9,8},{10,11... | collective-permute-start | bytes 1179656 | tf_op jit(solution)/shard_map/ppermute | solution.py:22
  5.8 27.7 %all-to-all-start = ((bf16[2,2,256,384]{3,1,0,2:T(2,128)(2,1)}), bf16[2,2,256,384]{3,1,0,2:T(2,128)(2,1)}, u32[]{:S(2)}, u32[]{:S(2)}) async-start(bf16[2,2,256,384]{3,1,0,2:T(2,128)(2,1)} %pad_maximum_fusion), calls=%async_computation | async-start | bytes 1572864 | tf_op jit(solution)/shard_map/all_to_all | solution.py:243
  23.4 11.8 %copy-start.49 = (bf16[2,256,1,1,64]{1,0,4,3,2:T(2,128)(2,1)}, bf16[2,256,1,1,64]{1,0,4,3,2:T(2,128)(2,1)S(1)}, u32[]{:S(2)}) copy-start(bf16[2,256,1,1,64]{1,0,4,3,2:T(2,128)(2,1)S(1)} %get-tuple-element.30) | copy-start | bytes 196612
  23.4 13.8 %copy-start.47 = (bf16[2,256,1,1,64]{1,0,4,3,2:T(2,128)(2,1)}, bf16[2,256,1,1,64]{1,0,4,3,2:T(2,128)(2,1)S(1)}, u32[]{:S(2)}) copy-start(bf16[2,256,1,1,64]{1,0,4,3,2:T(2,128)(2,1)S(1)} %get-tuple-element.27) | copy-start | bytes 196612
  23.4 17.8 %copy-start.45 = (bf16[2,256,1,1,64]{1,0,4,3,2:T(2,128)(2,1)}, bf16[2,256,1,1,64]{1,0,4,3,2:T(2,128)(2,1)S(1)}, u32[]{:S(2)}) copy-start(bf16[2,256,1,1,64]{1,0,4,3,2:T(2,128)(2,1)S(1)} %get-tuple-element.42) | copy-start | bytes 196612
  34.8 18.8 %collective-permute-start = (bf16[2,32,16,384]{3,2,1,0:T(8,128)(2,1)S(1)}, bf16[2,32,16,384]{3,2,1,0:T(8,128)(2,1)S(1)}, u32[]{:S(2)}, u32[]{:S(2)}) collective-permute-start(bf16[2,32,16,384]{3,2,1,0:T(8,128)(2,1)S(1)} %bitcast.639), channel_id=1, source_target_pairs={{0,1},{1,0},{2,3},{3,2},{4,5},{5,4},{6,7},{7,6},{8,9},{9,8},{10,11... | collective-permute-start | bytes 2359304 | tf_op jit(solution)/shard_map/ppermute | solution.py:22
  72.4 9.5 %copy-start.24 = (bf16[32,16,1,1,64]{4,3,2,1,0:T(2,128)(2,1)}, bf16[32,16,1,1,64]{4,3,2,1,0:T(2,128)(2,1)S(1)}, u32[]{:S(2)}) copy-start(bf16[32,16,1,1,64]{4,3,2,1,0:T(2,128)(2,1)S(1)} %get-tuple-element.16) | copy-start | bytes 196612
  72.4 20.0 %copy-start.22 = (bf16[32,16,1,1,64]{4,3,2,1,0:T(2,128)(2,1)}, bf16[32,16,1,1,64]{4,3,2,1,0:T(2,128)(2,1)S(1)}, u32[]{:S(2)}) copy-start(bf16[32,16,1,1,64]{4,3,2,1,0:T(2,128)(2,1)S(1)} %get-tuple-element.13) | copy-start | bytes 196612
  72.4 29.4 %copy-start.20 = (bf16[32,16,1,1,64]{4,3,2,1,0:T(2,128)(2,1)}, bf16[32,16,1,1,64]{4,3,2,1,0:T(2,128)(2,1)S(1)}, u32[]{:S(2)}) copy-start(bf16[32,16,1,1,64]{4,3,2,1,0:T(2,128)(2,1)S(1)} %get-tuple-element.10) | copy-start | bytes 196612
  72.4 38.8 %copy-start.18 = (bf16[32,16,1,1,64]{4,3,2,1,0:T(2,128)(2,1)}, bf16[32,16,1,1,64]{4,3,2,1,0:T(2,128)(2,1)S(1)}, u32[]{:S(2)}) copy-start(bf16[32,16,1,1,64]{4,3,2,1,0:T(2,128)(2,1)S(1)} %get-tuple-element.7) | copy-start | bytes 196612
  72.4 47.1 %copy-start.16 = (bf16[32,16,1,1,64]{4,3,2,1,0:T(2,128)(2,1)}, bf16[32,16,1,1,64]{4,3,2,1,0:T(2,128)(2,1)S(1)}, u32[]{:S(2)}) copy-start(bf16[32,16,1,1,64]{4,3,2,1,0:T(2,128)(2,1)S(1)} %get-tuple-element.22) | copy-start | bytes 196612
  127.5 9.5 %collective-permute-start.1 = (bf16[512,384]{1,0:T(8,128)(2,1)S(1)}, bf16[512,384]{1,0:T(8,128)(2,1)S(1)}, u32[]{:S(2)}, u32[]{:S(2)}) collective-permute-start(bf16[512,384]{1,0:T(8,128)(2,1)S(1)} %select_convert_fusion.1), channel_id=1, source_target_pairs={{0,1},{1,0},{2,3},{3,2},{4,5},{5,4},{6,7},{7,6},{8,9},{9,8},{10,11... | collective-permute-start | bytes 1179656 | tf_op jit(solution)/shard_map/ppermute | solution.py:22
  132.0 13.8 %copy-start.23 = (bf16[32,16,1,1,64]{4,3,2,1,0:T(2,128)(2,1)S(1)}, bf16[32,16,1,1,64]{4,3,2,1,0:T(2,128)(2,1)}, u32[]{:S(2)}) copy-start(bf16[32,16,1,1,64]{4,3,2,1,0:T(2,128)(2,1)} %copy-done.22) | copy-start | bytes 196612
  137.9 18.7 %all-to-all-start.1 = ((bf16[32,16,384]{2,1,0:T(8,128)(2,1)}), bf16[32,16,384]{2,1,0:T(8,128)(2,1)S(1)}, u32[]{:S(2)}, u32[]{:S(2)}) async-start(bf16[32,16,384]{2,1,0:T(8,128)(2,1)} %bitcast.50), calls=%async_computation.1 | async-start | bytes 786432 | tf_op jit(solution)/shard_map/all_to_all | solution.py:249
  156.7 19.7 %copy-start.7 = (bf16[2,256,384]{2,1,0:T(8,128)(2,1)}, bf16[2,256,384]{2,1,0:T(8,128)(2,1)S(1)}, u32[]{:S(2)}) copy-start(bf16[2,256,384]{2,1,0:T(8,128)(2,1)S(1)} %fusion.191) | copy-start | bytes 1179652
  156.7 10.7 %collective-permute-start.3 = (bf16[2,256,384]{2,1,0:T(8,128)(2,1)S(1)}, bf16[2,256,384]{2,1,0:T(8,128)(2,1)}, u32[]{:S(2)}, u32[]{:S(2)}) collective-permute-start(bf16[2,256,384]{2,1,0:T(8,128)(2,1)S(1)} %fusion.191), channel_id=1, source_target_pairs={{0,1},{1,0},{2,3},{3,2},{4,5},{5,4},{6,7},{7,6},{8,9},{9,8},{10,11... | collective-permute-start | bytes 1179656 | tf_op jit(solution)/shard_map/ppermute | solution.py:22
  159.3 20.0 %all-to-all-start.5 = ((bf16[16,48,384]{2,1,0:T(8,128)(2,1)}), bf16[16,48,384]{2,1,0:T(8,128)(2,1)S(1)}, u32[]{:S(2)}, u32[]{:S(2)}) async-start(bf16[16,48,384]{2,1,0:T(8,128)(2,1)} %bitcast.97), calls=%async_computation.5 | async-start | bytes 1179648 | tf_op jit(solution)/shard_map/all_to_all | solution.py:234
  170.4 20.0 %copy-start.60 = (bf16[2,256,1,64]{1,0,3,2:T(2,128)(2,1)}, bf16[2,256,1,64]{1,0,3,2:T(2,128)(2,1)S(1)}, u32[]{:S(2)}) copy-start(bf16[2,256,1,64]{1,0,3,2:T(2,128)(2,1)S(1)} %get-tuple-element.52) | copy-start | bytes 196612
  179.2 20.7 %all-to-all-start.3 = ((bf16[16,48,384]{2,1,0:T(8,128)(2,1)}), bf16[16,48,384]{2,1,0:T(8,128)(2,1)S(1)}, u32[]{:S(2)}, u32[]{:S(2)}) async-start(bf16[16,48,384]{2,1,0:T(8,128)(2,1)} %bitcast.87), calls=%async_computation.3 | async-start | bytes 1179648 | tf_op jit(solution)/shard_map/all_to_all | solution.py:234
  200.8 45.6 %all-to-all-start.4 = ((bf16[16,48,1152]{2,1,0:T(8,128)(2,1)}), bf16[16,48,1152]{2,1,0:T(8,128)(2,1)S(1)}, u32[]{:S(2)}, u32[]{:S(2)}) async-start(bf16[16,48,1152]{2,1,0:T(8,128)(2,1)} %bitcast.641), calls=%async_computation.4 | async-start | bytes 3538944 | tf_op jit(solution)/shard_map/all_to_all | solution.py:234
  246.4 45.5 %all-to-all-start.2 = ((bf16[16,48,1152]{2,1,0:T(8,128)(2,1)}), bf16[16,48,1152]{2,1,0:T(8,128)(2,1)}, u32[]{:S(2)}, u32[]{:S(2)}) async-start(bf16[16,48,1152]{2,1,0:T(8,128)(2,1)} %bitcast.85), calls=%async_computation.2 | async-start | bytes 3538944 | tf_op jit(solution)/shard_map/all_to_all | solution.py:234
  256.0 10.4 %collective-permute-start.4 = (bf16[512,384]{1,0:T(8,128)(2,1)S(1)}, bf16[512,384]{1,0:T(8,128)(2,1)S(1)}, u32[]{:S(2)}, u32[]{:S(2)}) collective-permute-start(bf16[512,384]{1,0:T(8,128)(2,1)S(1)} %select_convert_fusion), channel_id=1, source_target_pairs={{0,1},{1,0},{2,3},{3,2},{4,5},{5,4},{6,7},{7,6},{8,9},{9,8},{10,11... | collective-permute-start | bytes 1179656 | tf_op jit(solution)/shard_map/ppermute | solution.py:22
  268.4 26.0 %copy-start.1 = (bf16[768,1152]{1,0:T(8,128)(2,1)S(1)}, bf16[768,1152]{1,0:T(8,128)(2,1)}, u32[]{:S(2)}) copy-start(bf16[768,1152]{1,0:T(8,128)(2,1)} %param.12) | copy-start | bytes 5308420
  (84 other events, 261.9 us)

commit v2 on v0

--- a/solution.py
+++ b/solution.py
@@ -1,6 +1,10 @@
+import functools
+
 import jax
 import jax.numpy as jnp
 from jax import lax
+from jax.experimental import pallas as pl
+from jax.experimental.pallas import tpu as pltpu
 from jax.sharding import PartitionSpec as P
 
 HD = 64
@@ -176,6 +180,513 @@
     return (input_grad, qkv_doppler_grad, out_doppler_grad, qkv_range_grad, out_range_grad)
 
 
+MESH = pl.DeviceIdType.MESH
+F32 = jnp.float32
+BF16 = jnp.bfloat16
+PLAIN = (((1,), (0,)), ((), ()))
+HIDDEN = -1e30
+
+
+def mm(a, b, form=PLAIN):
+    return lax.dot_general(a, b, form, preferred_element_type=F32)
+
+
+def attention_unit(query, keys, values, grad_attn, seq_mask):
+    scale = HD ** (-0.5)
+    scores = mm(query, keys, TAIL_CONTRACT) * scale
+    if seq_mask is not None:
+        scores = jnp.where(seq_mask, scores, HIDDEN)
+    expo = jnp.exp(scores - jnp.max(scores, axis=-1, keepdims=True))
+    probs = expo * (1.0 / jnp.sum(expo, axis=-1, keepdims=True))
+    probs_low = probs.astype(BF16)
+    attended = mm(probs_low, values)
+    grad_values = mm(probs_low, grad_attn, LEAD_CONTRACT)
+    grad_probs = mm(grad_attn, values, TAIL_CONTRACT)
+    dots = jnp.sum(probs * grad_probs, axis=-1, keepdims=True)
+    grad_scores = (probs * (grad_probs - dots) * scale).astype(BF16)
+    grad_query = mm(grad_scores, keys)
+    grad_keys = mm(grad_scores, query, LEAD_CONTRACT)
+    return attended, (grad_query, grad_keys, grad_values)
+
+
+def layer_kernel(
+    seq,
+    dop_ref,
+    rng_ref,
+    cot_ref,
+    wqd_hbm,
+    wod_hbm,
+    wqr_hbm,
+    wor_hbm,
+    ig_ref,
+    qd_ref,
+    od_ref,
+    qr_ref,
+    or_ref,
+    wq,
+    wo,
+    xr,
+    xs,
+    xt,
+    pj32,
+    ga32,
+    pj,
+    ga,
+    gp,
+    att,
+    keep,
+    psend,
+    precv,
+    order,
+    rb,
+    back,
+    mid,
+    gs,
+    t1r,
+    t1,
+    t2r,
+    t2,
+    t3r,
+    wsem,
+    lsem,
+    a2a_s,
+    a2a_r,
+    fwd_s,
+    fwd_r,
+    dx_sem,
+    part_sem,
+    back_s,
+    back_r,
+    mid_sem,
+    rs12,
+    rs3_s,
+    rs3_r,
+):
+    s = lax.axis_index("seq")
+    h = lax.axis_index("head")
+    o = 1 - h
+    rows, bins, half = rng_ref.shape
+    span = bins // seq
+    tokens = rows * bins
+    block = tokens // 2
+    pair = {"seq": s, "head": o}
+    cols = wqr_hbm.shape[1]
+    tiles = cols // half
+
+    def at_seq(q):
+        return {"seq": q, "head": h}
+
+    def remote(src, dst, send, recv, where):
+        return pltpu.make_async_remote_copy(
+            src_ref=src,
+            dst_ref=dst,
+            send_sem=send,
+            recv_sem=recv,
+            device_id=(where["seq"], where["head"]),
+            device_id_type=MESH,
+        )
+
+    loads = [
+        pltpu.make_async_copy(wqr_hbm, wq.at[0], wsem.at[0]),
+        pltpu.make_async_copy(wor_hbm, wo.at[0], wsem.at[1]),
+        pltpu.make_async_copy(wqd_hbm, wq.at[1], wsem.at[2]),
+        pltpu.make_async_copy(wod_hbm, wo.at[1], wsem.at[3]),
+    ]
+    for load in loads:
+        load.start()
+
+    barrier = pltpu.get_barrier_semaphore()
+
+    @pl.loop(1, seq)
+    def _(k):
+        pl.semaphore_signal(
+            barrier, inc=1, device_id=(lax.rem(s + k, seq), h), device_id_type=MESH
+        )
+
+    pl.semaphore_signal(barrier, inc=1, device_id=(s, o), device_id_type=MESH)
+    pl.semaphore_wait(barrier, seq)
+
+    sources = (rng_ref, cot_ref)
+
+    def exchange(a, k):
+        peer = lax.rem(s + k, seq)
+        return remote(
+            sources[a].at[:, pl.ds(pl.multiple_of(peer * span, span), span), :],
+            xr.at[a, h, pl.ds(s * rows, rows)],
+            a2a_s.at[a, k],
+            a2a_r.at[a, k],
+            at_seq(peer),
+        )
+
+    def forward(a, k):
+        origin = lax.rem(s - k + seq, seq)
+        place = xr.at[a, h, pl.ds(origin * rows, rows)]
+        return remote(place, place, fwd_s.at[a, k], fwd_r.at[a, k], pair)
+
+    @pl.loop(1, seq)
+    def _(k):
+        for a in range(2):
+            exchange(a, k).start()
+
+    for a in range(2):
+        own = pltpu.make_async_copy(
+            sources[a].at[:, pl.ds(pl.multiple_of(s * span, span), span), :],
+            xr.at[a, h, pl.ds(s * rows, rows)],
+            lsem.at[a],
+        )
+        own.start()
+        own.wait()
+        forward(a, 0).start()
+
+    @pl.loop(1, seq)
+    def _(k):
+        for a in range(2):
+            exchange(a, k).wait_recv()
+            forward(a, k).start()
+
+    dop_send = remote(dop_ref, xs.at[1, 0, h], dx_sem.at[0], dx_sem.at[1], pair)
+    dop_send.start()
+    dop_own = pltpu.make_async_copy(dop_ref, xs.at[1, 0, h], lsem.at[2])
+    dop_own.start()
+
+    def to_blocks(side):
+        for a in range(2):
+            moved = xr[a, side].astype(F32)
+            for b in range(2):
+                piece = moved[:, b * (span // 2) : (b + 1) * (span // 2), :]
+                xs[0, a, side, b * block : (b + 1) * block, :] = piece.reshape(
+                    block, half
+                ).astype(BF16)
+
+    def turn(sub, a, side):
+        xt[sub, a, side] = xs[sub, a, side].T
+
+    def project(sub, side, first):
+        @pl.loop(0, tiles)
+        def _(t):
+            at = pl.ds(pl.multiple_of(t * half, half), half)
+            term = mm(xs[sub, 0, side], wq[sub, pl.ds(pl.multiple_of(side * half, half), half), at])
+            if first:
+                pj32[:, at] = term
+            else:
+                pj[:, at] = (pj32[:, at] + term).astype(BF16)
+
+    def project_cot(sub, side, first):
+        at = pl.ds(pl.multiple_of(side * half, half), half)
+        term = mm(xs[sub, 1, side], wo[sub, :, at], TAIL_CONTRACT)
+        if first:
+            ga32[...] = term
+        else:
+            ga[...] = (ga32[...] + term).astype(BF16)
+
+    def attention(seq_mask):
+        @pl.loop(0, tiles)
+        def _(t):
+            at = pl.ds(pl.multiple_of(t * half, half), half)
+            at_out = pl.ds(pl.multiple_of(t * 2 * HD, 2 * HD), 2 * HD)
+            for b in range(2):
+                here = slice(b * block, (b + 1) * block)
+                six = pj[here, at]
+                two = ga[here, at_out]
+                att_list, grad_list = [], []
+                for i in range(2):
+                    q, k, v = [six[:, (3 * i + j) * HD : (3 * i + j + 1) * HD] for j in range(3)]
+                    attended, grads = attention_unit(
+                        q, k, v, two[:, i * HD : (i + 1) * HD], seq_mask
+                    )
+                    att_list.append(attended)
+                    grad_list += list(grads)
+                att[here, at_out] = jnp.concatenate(att_list, -1).astype(BF16)
+                gp[here, at] = jnp.concatenate(grad_list, -1).astype(BF16)
+
+    def part_of(sub, side):
+        return mm(gp[...], wq[sub, pl.ds(pl.multiple_of(side * half, half), half), :], TAIL_CONTRACT)
+
+    def part_exchange(sub):
+        return remote(
+            psend.at[sub], precv.at[sub], part_sem.at[sub, 0], part_sem.at[sub, 1], pair
+        )
+
+    core = lax.rem(s, 2)
+    xbit = lax.rem(s // 2, 2)
+    z = s // 4
+    zs = seq // 4
+    chunk = 2 * half // seq
+    width = cols + half
+
+    def grads(sub):
+        @pl.loop(0, tiles)
+        def _(t):
+            at = pl.ds(pl.multiple_of(t * half, half), half)
+            for side in range(2):
+                term = mm(xt[sub, 0, side], gp[:, at]).astype(BF16)
+                gs[sub, side, :, :, :, at] = term.reshape(seq // 4, 2, chunk, half)
+
+        for side in range(2):
+            term = mm(xt[sub, 1, side], att[...]).astype(BF16)
+            gs[sub, side, :, :, :, cols:] = term.reshape(seq // 4, 2, chunk, half)
+
+    def rs_first(sub):
+        return remote(
+            gs.at[sub, :, :, 1 - core],
+            t1r.at[sub],
+            rs12.at[sub, 0],
+            rs12.at[sub, 1],
+            at_seq(s + 1 - 2 * core),
+        )
+
+    def rs_second(sub):
+        return remote(
+            t1.at[sub, :, 1 - xbit],
+            t2r.at[sub],
+            rs12.at[sub, 2],
+            rs12.at[sub, 3],
+            at_seq(s + 2 - 4 * xbit),
+        )
+
+    def rs_third(sub, k):
+        to = lax.rem(z + k, zs)
+        return remote(
+            t2.at[sub, to],
+            t3r.at[sub, k - 1],
+            rs3_s.at[sub, k - 1],
+            rs3_r.at[sub, k - 1],
+            at_seq(to * 4 + lax.rem(s, 4)),
+        )
+
+    def rs_after_first(sub):
+        rs_first(sub).wait_recv()
+        for side in range(2):
+
+            @pl.loop(0, seq // 4)
+            def _(c):
+                at = side * (seq // 4) + c
+                total = gs[sub, side, c, core].astype(F32) + t1r[sub, side, c].astype(F32)
+                t1[sub, at // 2, lax.rem(at, 2)] = total.astype(BF16)
+
+        rs_second(sub).start()
+
+    def rs_after_second(sub):
+        rs_second(sub).wait_recv()
+
+        @pl.loop(0, zs)
+        def _(c):
+            total = t1[sub, c, xbit].astype(F32) + t2r[sub, c].astype(F32)
+            t2[sub, c] = total.astype(BF16)
+
+        for k in range(1, zs):
+            rs_third(sub, k).start()
+
+    def rs_finish(sub, q_out, o_out):
+        total = t2[sub, z].astype(F32)
+        for k in range(1, zs):
+            rs_third(sub, k).wait_recv()
+            total = total + t3r[sub, k - 1].astype(F32)
+        q_out[...] = total[:, :cols]
+        o_out[...] = total[:, cols:]
+
+    loads[0].wait()
+    loads[1].wait()
+    to_blocks(h)
+    project(0, h, True)
+    project_cot(0, h, True)
+    turn(0, 0, h)
+    turn(0, 1, h)
+
+    @pl.loop(0, seq)
+    def _(k):
+        for a in range(2):
+            forward(a, k).wait_recv()
+
+    to_blocks(o)
+    project(0, o, False)
+    project_cot(0, o, False)
+    row_ids = lax.broadcasted_iota(jnp.int32, (block, block), 0)
+    col_ids = lax.broadcasted_iota(jnp.int32, (block, block), 1)
+    lane = span // 2
+    attention(lax.rem(row_ids, lane) == lax.rem(col_ids, lane))
+    psend[0] = part_of(0, o).astype(BF16)
+    part_exchange(0).start()
+    keep[...] = part_of(0, h)
+    turn(0, 0, o)
+    turn(0, 1, o)
+    part_exchange(0).wait_recv()
+    for b in range(2):
+        here = slice(b * block, (b + 1) * block)
+        total = keep[here, :] + precv[0, here, :].astype(F32)
+        order[:, b * lane : (b + 1) * lane, :] = total.reshape(block // lane, lane, half)
+    rb[...] = order[...].astype(BF16)
+
+    def give_back(k):
+        peer = lax.rem(s + k, seq)
+        return remote(
+            rb.at[pl.ds(peer * rows, rows)],
+            back.at[:, pl.ds(pl.multiple_of(s * span, span), span), :],
+            back_s.at[k],
+            back_r.at[k],
+            at_seq(peer),
+        )
+
+    @pl.loop(1, seq)
+    def _(k):
+        give_back(k).start()
+
+    back_own = pltpu.make_async_copy(
+        rb.at[pl.ds(s * rows, rows)],
+        back.at[:, pl.ds(pl.multiple_of(s * span, span), span), :],
+        lsem.at[3],
+    )
+    back_own.start()
+    grads(0)
+    back_own.wait()
+
+    @pl.loop(1, seq)
+    def _(k):
+        give_back(k).wait_recv()
+
+    for r in range(rows):
+        new = cot_ref[r].astype(F32) + back[r].astype(F32)
+        mid[r * bins : (r + 1) * bins, :] = new.astype(BF16)
+    mid_send = remote(mid, xs.at[1, 1, h], mid_sem.at[0], mid_sem.at[1], pair)
+    mid_send.start()
+    rs_first(0).start()
+    xs[1, 1, h] = mid[...]
+    loads[2].wait()
+    loads[3].wait()
+    dop_own.wait()
+    project(1, h, True)
+    project_cot(1, h, True)
+    dop_send.wait_recv()
+    project(1, o, False)
+    rs_after_first(0)
+    for side in range(2):
+        turn(1, 0, side)
+    turn(1, 1, h)
+    mid_send.wait_recv()
+    project_cot(1, o, False)
+    rs_after_second(0)
+    attention(None)
+    turn(1, 1, o)
+    grads(1)
+    rs_first(1).start()
+    psend[1] = part_of(1, o).astype(BF16)
+    part_exchange(1).start()
+    rs_after_first(1)
+    keep[...] = part_of(1, h)
+    rs_finish(0, qr_ref, or_ref)
+    part_exchange(1).wait_recv()
+    added = (keep[...] + precv[1].astype(F32)).astype(BF16).astype(F32)
+    ig_ref[...] = (mid[...].astype(F32) + added).astype(BF16)
+    rs_after_second(1)
+    rs_finish(1, qd_ref, od_ref)
+
+    @pl.loop(1, seq)
+    def _(k):
+        for a in range(2):
+            exchange(a, k).wait_send()
+        give_back(k).wait_send()
+
+    @pl.loop(0, seq)
+    def _(k):
+        for a in range(2):
+            forward(a, k).wait_send()
+
+    dop_send.wait_send()
+    mid_send.wait_send()
+    for sub in range(2):
+        part_exchange(sub).wait_send()
+        rs_first(sub).wait_send()
+        rs_second(sub).wait_send()
+        for k in range(1, zs):
+            rs_third(sub, k).wait_send()
+
+
+def shards_by_head(
+    doppler_input, range_saved_input, layer_cot, qkv_doppler, out_doppler, qkv_range, out_range
+):
+    seq = lax.axis_size("seq")
+    rows, bins, half = layer_cot.shape
+    tokens = rows * bins
+    cols = qkv_range.shape[1]
+    chunk = 2 * half // seq
+    width = cols + half
+    span = bins // seq
+    dma = pltpu.SemaphoreType.DMA
+    vmem = pl.BlockSpec(memory_space=pltpu.VMEM)
+    hbm = pl.BlockSpec(memory_space=pl.ANY)
+    zs = seq // 4
+    scratch = [
+        pltpu.VMEM((2, 2 * half, cols), BF16),
+        pltpu.VMEM((2, half, 2 * half), BF16),
+        pltpu.VMEM((2, 2, rows * seq, span, half), BF16),
+        pltpu.VMEM((2, 2, 2, tokens, half), BF16),
+        pltpu.VMEM((2, 2, 2, half, tokens), BF16),
+        pltpu.VMEM((tokens, cols), F32),
+        pltpu.VMEM((tokens, half), F32),
+        pltpu.VMEM((tokens, cols), BF16),
+        pltpu.VMEM((tokens, half), BF16),
+        pltpu.VMEM((tokens, cols), BF16),
+        pltpu.VMEM((tokens, half), BF16),
+        pltpu.VMEM((tokens, half), F32),
+        pltpu.VMEM((2, tokens, half), BF16),
+        pltpu.VMEM((2, tokens, half), BF16),
+        pltpu.VMEM((rows * seq, span, half), F32),
+        pltpu.VMEM((rows * seq, span, half), BF16),
+        pltpu.VMEM((rows, bins, half), BF16),
+        pltpu.VMEM((tokens, half), BF16),
+        pltpu.VMEM((2, 2, seq // 4, 2, chunk, width), BF16),
+        pltpu.VMEM((2, 2, seq // 4, chunk, width), BF16),
+        pltpu.VMEM((2, zs, 2, chunk, width), BF16),
+        pltpu.VMEM((2, zs, chunk, width), BF16),
+        pltpu.VMEM((2, zs, chunk, width), BF16),
+        pltpu.VMEM((2, zs - 1, chunk, width), BF16),
+        dma((4,)),
+        dma((4,)),
+        dma((2, seq)),
+        dma((2, seq)),
+        dma((2, seq)),
+        dma((2, seq)),
+        dma((2,)),
+        dma((2, 2)),
+        dma((seq,)),
+        dma((seq,)),
+        dma((2,)),
+        dma((2, 4)),
+        dma((2, zs - 1)),
+        dma((2, zs - 1)),
+    ]
+    ig, qd, od, qr, out_r = pl.pallas_call(
+        functools.partial(layer_kernel, seq),
+        out_shape=(
+            jax.ShapeDtypeStruct((tokens, half), BF16),
+            jax.ShapeDtypeStruct((chunk, cols), F32),
+            jax.ShapeDtypeStruct((chunk, half), F32),
+            jax.ShapeDtypeStruct((chunk, cols), F32),
+            jax.ShapeDtypeStruct((chunk, half), F32),
+        ),
+        in_specs=[vmem] * 3 + [hbm] * 4,
+        out_specs=(vmem,) * 5,
+        scratch_shapes=scratch,
+        compiler_params=pltpu.CompilerParams(
+            collective_id=0, has_side_effects=True, vmem_limit_bytes=56 * 2**20
+        ),
+        name="axial_backward",
+    )(
+        doppler_input.reshape(tokens, half),
+        range_saved_input,
+        layer_cot,
+        qkv_doppler,
+        out_doppler,
+        qkv_range,
+        out_range,
+    )
+    return (ig.reshape(layer_cot.shape), qd, od.T, qr, out_r.T)
+
+
+def by_head(mesh):
+    return mesh.shape["head"] == 2 and mesh.shape["seq"] == 16
+
+
 def solution(mesh):
     placed = (
         P("seq", None, "head"),
@@ -187,7 +698,7 @@
         P("head", None),
     )
     return jax.shard_map(
-        shards,
+        shards_by_head if by_head(mesh) else shards,
         mesh=mesh,
         in_specs=placed,
         out_specs=(

time: 617 us -> 133 us (0.22)
  waiting for transfers between devices: 216 us -> 0 us
  blocking collectives: 154 us -> 0 us
  Pallas kernels: 0 us -> 124 us
  matrix products: 112 us -> 0 us
  local copies, waits for them, and re-layouts: 58.4 us -> 7.24 us
  starting transfers between devices: 29.1 us -> 0 us
  other arithmetic: 23.3 us -> 0 us
  between operations: 16.8 us -> 0.65 us
    all_gather x4 -> x0, blocking collectives: 146 us -> none  [the longest x1 109 us: shards(): lax.all_gather(doppler_input, 'head', axis=2, tiled=True)]
    reduce_scatter x2 -> x0, waiting for transfers between devices: 140 us -> none  [reduction_terms(): lax.psum_scatter(qkv_term, 'seq', scatter_dimension=0, tiled=True)]
    pallas_call x0 -> x1, Pallas kernels: none -> 124 us  [shards_by_head(): pl.pallas_call(functools.partial(layer_kernel, seq), out_shape=(jax.Shape...]
    dot_general x142 -> x0, matrix products: 108 us -> none  [the longest x12 15.8 us: head_backward(): jnp.einsum(forms[0], query, keys, preferred_element_type=jnp.float32)]
    ppermute x8 -> x0, waiting for transfers between devices: 49.6 us -> none  [swapped(): return lax.ppermute(block, axis, route)]
    all_to_all x4 -> x0, waiting for transfers between devices: 26.4 us -> none  [the longest x1 16.8 us: shards(): lax.all_to_all(range_part, 'head', split_axis=2, concat_axis=1, tiled=True)]
    all_to_all x4 -> x0, starting transfers between devices: 21.3 us -> none  [the longest x1 6.16 us: shards(): lax.all_to_all(full_mid, 'seq', split_axis=1, concat_axis=0, tiled=True)]
    reshape x6 -> x0, local copies, waits for them, and re-layouts: 17.9 us -> none  [the longest x1 6.34 us: sublayer_local(): grad_proj = jnp.stack(grad_list, axis=-3).reshape(-1, 3 * heads_here * HD)]
  transfers between devices with their start and end apart: 16 -> 0, of which waited for: 7 -> 0; matrix products, arithmetic and copies ran while one was open for 30% -> 0% of each run, Pallas kernels for 0% -> 0%
where the time goes in v2:
time: 133 us; the launch traced here: 132 us
  Pallas kernels  124 us (93%)
  local copies, waits for them, and re-layouts  7.24 us (5%)
    pallas_call x1, Pallas kernels, shards_by_head(): pl.pallas_call(functools.partial(layer_kernel, seq), out_shape=(jax.Shape...  124 us
    unnamed x7, local copies, waits for them, and re-layouts  7.24 us

profile of v2, /device:TPU:0, one launch (start us, length us, event | category | flops | bytes accessed | tf_op | source)
XLA Modules:
  0.0 131.5 jit_solution(16986459089598185998)
XLA Ops:
  0.6 123.6 %axial_backward.1 = (bf16[512,384]{1,0:T(8,128)(2,1)}, f32[48,1152]{1,0:T(8,128)}, f32[48,384]{1,0:T(8,128)}, f32[48,1152]{1,0:T(8,128)}, f32[48,384]{1,0:T(8,128)}) custom-call(bf16[512,384]{1,0:T(8,128)(2,1)} %bitcast.4, bf16[2,256,384]{2,1,0:T(8,128)(2,1)} %rng_ref.1, bf16[2,256,384]{2,1,0:T(8,128)(2,1)} %cot_ref.1, bf16[768,1152]{1,0:T(8,128)(2,1)} %wqd_hbm.1, ...), custom_call_target="tpu_custom_call" | custom-call | tf_op jit(solution)/shard_map/axial_backward/pallas_call | solution.py:658
  124.3 0.0 copy-start
  124.3 1.8 %copy.17 = bf16[2,256,384]{2,1,0:T(8,128)(2,1)} copy(bf16[2,256,384]{2,1,0:T(8,128)(2,1)} %bitcast.5) | data formatting | bytes 786432
  126.1 1.6 %copy.18 = f32[48,1152]{1,0:T(8,128)} copy(f32[48,1152]{1,0:T(8,128)} %get-tuple-element.21) | data formatting | bytes 442368
  127.7 1.5 %copy.19 = f32[384,48]{0,1:T(8,128)} copy(f32[384,48]{0,1:T(8,128)} %bitcast.7) | data formatting | bytes 147456
  129.3 1.6 %copy.20 = f32[48,1152]{1,0:T(8,128)} copy(f32[48,1152]{1,0:T(8,128)} %get-tuple-element.23) | data formatting | bytes 442368
  130.9 0.0 copy-done
  130.9 0.6 copy.21
Async XLA Ops:
  124.3 6.6 %copy-start = (f32[48,384]{1,0:T(8,128)S(1)}, f32[48,384]{1,0:T(8,128)}, u32[]{:S(2)}) copy-start(f32[48,384]{1,0:T(8,128)} %get-tuple-element.14) | copy-start | bytes 221188

commit v3 on v2

--- a/solution.py
+++ b/solution.py
@@ -272,6 +272,9 @@
     pair = {"seq": s, "head": o}
     cols = wqr_hbm.shape[1]
     tiles = cols // half
+    lanes = 128
+    cuts = half // lanes
+    pieces = tiles + 1
 
     def at_seq(q):
         return {"seq": q, "head": h}
@@ -379,111 +382,112 @@
         else:
             ga[...] = (ga32[...] + term).astype(BF16)
 
-    def attention(seq_mask):
-        @pl.loop(0, tiles)
-        def _(t):
-            at = pl.ds(pl.multiple_of(t * half, half), half)
-            at_out = pl.ds(pl.multiple_of(t * 2 * HD, 2 * HD), 2 * HD)
-            for b in range(2):
-                here = slice(b * block, (b + 1) * block)
-                six = pj[here, at]
-                two = ga[here, at_out]
-                att_list, grad_list = [], []
-                for i in range(2):
-                    q, k, v = [six[:, (3 * i + j) * HD : (3 * i + j + 1) * HD] for j in range(3)]
-                    attended, grads = attention_unit(
-                        q, k, v, two[:, i * HD : (i + 1) * HD], seq_mask
-                    )
-                    att_list.append(attended)
-                    grad_list += list(grads)
-                att[here, at_out] = jnp.concatenate(att_list, -1).astype(BF16)
-                gp[here, at] = jnp.concatenate(grad_list, -1).astype(BF16)
-
-    def part_of(sub, side):
-        return mm(gp[...], wq[sub, pl.ds(pl.multiple_of(side * half, half), half), :], TAIL_CONTRACT)
-
-    def part_exchange(sub):
+    def attention(t, seq_mask):
+        at = pl.ds(pl.multiple_of(t * half, half), half)
+        at_out = pl.ds(pl.multiple_of(t * 2 * HD, 2 * HD), 2 * HD)
+        for b in range(2):
+            here = slice(b * block, (b + 1) * block)
+            six = pj[here, at]
+            two = ga[here, at_out]
+            att_list, grad_list = [], []
+            for i in range(2):
+                q, k, v = [six[:, (3 * i + j) * HD : (3 * i + j + 1) * HD] for j in range(3)]
+                attended, grads = attention_unit(q, k, v, two[:, i * HD : (i + 1) * HD], seq_mask)
+                att_list.append(attended)
+                grad_list += list(grads)
+            att[here, at_out] = jnp.concatenate(att_list, -1).astype(BF16)
+            gp[here, at] = jnp.concatenate(grad_list, -1).astype(BF16)
+
+    def part_of(sub, side, f):
+        at = pl.ds(pl.multiple_of(side * half + f * lanes, lanes), lanes)
+        return mm(gp[...], wq[sub, at, :], TAIL_CONTRACT)
+
+    def part_exchange(sub, f):
         return remote(
-            psend.at[sub], precv.at[sub], part_sem.at[sub, 0], part_sem.at[sub, 1], pair
-        )
+            psend.at[sub, f],
+            precv.at[sub, f],
+            part_sem.at[sub, f, 0],
+            part_sem.at[sub, f, 1],
+            pair,
+        )
+
+    def send_parts(sub):
+        for f in range(cuts):
+            psend[sub, f] = part_of(sub, o, f).astype(BF16)
+            part_exchange(sub, f).start()
+
+    def cut(f):
+        return slice(f * lanes, (f + 1) * lanes)
 
     core = lax.rem(s, 2)
     xbit = lax.rem(s // 2, 2)
     z = s // 4
     zs = seq // 4
     chunk = 2 * half // seq
-    width = cols + half
-
-    def grads(sub):
-        @pl.loop(0, tiles)
-        def _(t):
-            at = pl.ds(pl.multiple_of(t * half, half), half)
-            for side in range(2):
-                term = mm(xt[sub, 0, side], gp[:, at]).astype(BF16)
-                gs[sub, side, :, :, :, at] = term.reshape(seq // 4, 2, chunk, half)
-
+
+    def grads(sub, p):
+        if isinstance(p, int) and p == tiles:
+            a, right = 1, att[...]
+        else:
+            a, right = 0, gp[:, pl.ds(pl.multiple_of(p * half, half), half)]
         for side in range(2):
-            term = mm(xt[sub, 1, side], att[...]).astype(BF16)
-            gs[sub, side, :, :, :, cols:] = term.reshape(seq // 4, 2, chunk, half)
-
-    def rs_first(sub):
+            term = mm(xt[sub, a, side], right).astype(BF16)
+            gs[sub, p, side] = term.reshape(seq // 4, 2, chunk, half)
+
+    def rs_first(sub, p):
         return remote(
-            gs.at[sub, :, :, 1 - core],
-            t1r.at[sub],
-            rs12.at[sub, 0],
-            rs12.at[sub, 1],
+            gs.at[sub, p, :, :, 1 - core],
+            t1r.at[sub, p],
+            rs12.at[sub, p, 0],
+            rs12.at[sub, p, 1],
             at_seq(s + 1 - 2 * core),
         )
 
-    def rs_second(sub):
+    def rs_second(sub, p):
         return remote(
-            t1.at[sub, :, 1 - xbit],
-            t2r.at[sub],
-            rs12.at[sub, 2],
-            rs12.at[sub, 3],
+            t1.at[sub, p, :, 1 - xbit],
+            t2r.at[sub, p],
+            rs12.at[sub, p, 2],
+            rs12.at[sub, p, 3],
             at_seq(s + 2 - 4 * xbit),
         )
 
-    def rs_third(sub, k):
+    def rs_third(sub, p, k):
         to = lax.rem(z + k, zs)
         return remote(
-            t2.at[sub, to],
-            t3r.at[sub, k - 1],
-            rs3_s.at[sub, k - 1],
-            rs3_r.at[sub, k - 1],
+            t2.at[sub, p, to],
+            t3r.at[sub, p, k - 1],
+            rs3_s.at[sub, p, k - 1],
+            rs3_r.at[sub, p, k - 1],
             at_seq(to * 4 + lax.rem(s, 4)),
         )
 
-    def rs_after_first(sub):
-        rs_first(sub).wait_recv()
+    def rs_after_first(sub, p):
+        rs_first(sub, p).wait_recv()
         for side in range(2):
-
-            @pl.loop(0, seq // 4)
-            def _(c):
+            for c in range(seq // 4):
                 at = side * (seq // 4) + c
-                total = gs[sub, side, c, core].astype(F32) + t1r[sub, side, c].astype(F32)
-                t1[sub, at // 2, lax.rem(at, 2)] = total.astype(BF16)
-
-        rs_second(sub).start()
-
-    def rs_after_second(sub):
-        rs_second(sub).wait_recv()
-
-        @pl.loop(0, zs)
-        def _(c):
-            total = t1[sub, c, xbit].astype(F32) + t2r[sub, c].astype(F32)
-            t2[sub, c] = total.astype(BF16)
-
+                total = gs[sub, p, side, c, core].astype(F32) + t1r[sub, p, side, c].astype(F32)
+                t1[sub, p, at // 2, at % 2] = total.astype(BF16)
+        rs_second(sub, p).start()
+
+    def rs_after_second(sub, p):
+        rs_second(sub, p).wait_recv()
+        for c in range(zs):
+            total = t1[sub, p, c, xbit].astype(F32) + t2r[sub, p, c].astype(F32)
+            t2[sub, p, c] = total.astype(BF16)
         for k in range(1, zs):
-            rs_third(sub, k).start()
-
-    def rs_finish(sub, q_out, o_out):
-        total = t2[sub, z].astype(F32)
+            rs_third(sub, p, k).start()
+
+    def rs_finish(sub, p, q_out, o_out):
+        total = t2[sub, p, z].astype(F32)
         for k in range(1, zs):
-            rs_third(sub, k).wait_recv()
-            total = total + t3r[sub, k - 1].astype(F32)
-        q_out[...] = total[:, :cols]
-        o_out[...] = total[:, cols:]
+            rs_third(sub, p, k).wait_recv()
+            total = total + t3r[sub, p, k - 1].astype(F32)
+        if p == tiles:
+            o_out[...] = total
+        else:
+            q_out[:, p * half : (p + 1) * half] = total
 
     loads[0].wait()
     loads[1].wait()
@@ -504,87 +508,133 @@
     row_ids = lax.broadcasted_iota(jnp.int32, (block, block), 0)
     col_ids = lax.broadcasted_iota(jnp.int32, (block, block), 1)
     lane = span // 2
-    attention(lax.rem(row_ids, lane) == lax.rem(col_ids, lane))
-    psend[0] = part_of(0, o).astype(BF16)
-    part_exchange(0).start()
-    keep[...] = part_of(0, h)
+    seq_mask = lax.rem(row_ids, lane) == lax.rem(col_ids, lane)
+
+    @pl.loop(0, tiles)
+    def _(t):
+        attention(t, seq_mask)
+
+    send_parts(0)
+    for f in range(cuts):
+        keep[:, cut(f)] = part_of(0, h, f)
     turn(0, 0, o)
     turn(0, 1, o)
-    part_exchange(0).wait_recv()
-    for b in range(2):
-        here = slice(b * block, (b + 1) * block)
-        total = keep[here, :] + precv[0, here, :].astype(F32)
-        order[:, b * lane : (b + 1) * lane, :] = total.reshape(block // lane, lane, half)
-    rb[...] = order[...].astype(BF16)
-
-    def give_back(k):
+
+    def give_back(f, k):
         peer = lax.rem(s + k, seq)
         return remote(
-            rb.at[pl.ds(peer * rows, rows)],
-            back.at[:, pl.ds(pl.multiple_of(s * span, span), span), :],
-            back_s.at[k],
-            back_r.at[k],
+            rb.at[f, pl.ds(peer * rows, rows)],
+            back.at[f, :, pl.ds(pl.multiple_of(s * span, span), span), :],
+            back_s.at[f, k],
+            back_r.at[f, k],
             at_seq(peer),
         )
 
-    @pl.loop(1, seq)
-    def _(k):
-        give_back(k).start()
-
-    back_own = pltpu.make_async_copy(
-        rb.at[pl.ds(s * rows, rows)],
-        back.at[:, pl.ds(pl.multiple_of(s * span, span), span), :],
-        lsem.at[3],
-    )
-    back_own.start()
-    grads(0)
-    back_own.wait()
-
-    @pl.loop(1, seq)
-    def _(k):
-        give_back(k).wait_recv()
-
-    for r in range(rows):
-        new = cot_ref[r].astype(F32) + back[r].astype(F32)
-        mid[r * bins : (r + 1) * bins, :] = new.astype(BF16)
-    mid_send = remote(mid, xs.at[1, 1, h], mid_sem.at[0], mid_sem.at[1], pair)
-    mid_send.start()
-    rs_first(0).start()
-    xs[1, 1, h] = mid[...]
+    back_own = []
+    for f in range(cuts):
+        part_exchange(0, f).wait_recv()
+        for b in range(2):
+            here = slice(b * block, (b + 1) * block)
+            total = keep[here, cut(f)] + precv[0, f, here, :].astype(F32)
+            order[:, b * lane : (b + 1) * lane, :] = total.reshape(block // lane, lane, lanes)
+        rb[f] = order[...].astype(BF16)
+
+        @pl.loop(1, seq)
+        def _(k):
+            give_back(f, k).start()
+
+        back_own.append(
+            pltpu.make_async_copy(
+                rb.at[f, pl.ds(s * rows, rows)],
+                back.at[f, :, pl.ds(pl.multiple_of(s * span, span), span), :],
+                lsem.at[3 + f],
+            )
+        )
+        back_own[f].start()
+        grads(0, f)
+
+    def send_mid(f):
+        return remote(
+            mid.at[f], xs.at[1, 1, h, :, cut(f)], mid_sem.at[f, 0], mid_sem.at[f, 1], pair
+        )
+
+    for f in range(cuts):
+        back_own[f].wait()
+
+        @pl.loop(1, seq)
+        def _(k):
+            give_back(f, k).wait_recv()
+
+        for r in range(rows):
+            here = slice(r * bins, (r + 1) * bins)
+            new = (cot_ref[r, :, cut(f)].astype(F32) + back[f, r].astype(F32)).astype(BF16)
+            mid[f, here, :] = new
+            xs[1, 1, h, here, cut(f)] = new
+        send_mid(f).start()
+
+    for p in range(cuts, pieces):
+        grads(0, p)
+    for p in range(pieces):
+        rs_first(0, p).start()
     loads[2].wait()
     loads[3].wait()
     dop_own.wait()
     project(1, h, True)
     project_cot(1, h, True)
+    for p in range(pieces):
+        rs_after_first(0, p)
     dop_send.wait_recv()
     project(1, o, False)
-    rs_after_first(0)
     for side in range(2):
         turn(1, 0, side)
     turn(1, 1, h)
-    mid_send.wait_recv()
+    for f in range(cuts):
+        send_mid(f).wait_recv()
     project_cot(1, o, False)
-    rs_after_second(0)
-    attention(None)
+    for p in range(pieces):
+        rs_after_second(0, p)
+
+    @pl.loop(0, tiles)
+    def _(t):
+        attention(t, None)
+        grads(1, t)
+        rs_first(1, t).start()
+
+        @pl.when(t >= 1)
+        def _():
+            rs_after_first(1, t - 1)
+
+        @pl.when(t >= 2)
+        def _():
+            rs_after_second(1, t - 2)
+
+    send_parts(1)
+    rs_after_first(1, tiles - 1)
     turn(1, 1, o)
-    grads(1)
-    rs_first(1).start()
-    psend[1] = part_of(1, o).astype(BF16)
-    part_exchange(1).start()
-    rs_after_first(1)
-    keep[...] = part_of(1, h)
-    rs_finish(0, qr_ref, or_ref)
-    part_exchange(1).wait_recv()
-    added = (keep[...] + precv[1].astype(F32)).astype(BF16).astype(F32)
-    ig_ref[...] = (mid[...].astype(F32) + added).astype(BF16)
-    rs_after_second(1)
-    rs_finish(1, qd_ref, od_ref)
+    grads(1, tiles)
+    rs_first(1, tiles).start()
+    for f in range(cuts):
+        keep[:, cut(f)] = part_of(1, h, f)
+    for p in range(max(tiles - 2, 0), tiles - 1):
+        rs_after_second(1, p)
+    rs_after_first(1, tiles)
+    for p in range(pieces):
+        rs_finish(0, p, qr_ref, or_ref)
+    for p in range(tiles - 1, pieces):
+        rs_after_second(1, p)
+    for f in range(cuts):
+        part_exchange(1, f).wait_recv()
+        added = (keep[:, cut(f)] + precv[1, f].astype(F32)).astype(BF16).astype(F32)
+        ig_ref[:, cut(f)] = (mid[f].astype(F32) + added).astype(BF16)
+    for p in range(pieces):
+        rs_finish(1, p, qd_ref, od_ref)
 
     @pl.loop(1, seq)
     def _(k):
         for a in range(2):
             exchange(a, k).wait_send()
-        give_back(k).wait_send()
+        for f in range(cuts):
+            give_back(f, k).wait_send()
 
     @pl.loop(0, seq)
     def _(k):
@@ -592,13 +642,24 @@
             forward(a, k).wait_send()
 
     dop_send.wait_send()
-    mid_send.wait_send()
+    for f in range(cuts):
+        send_mid(f).wait_send()
     for sub in range(2):
-        part_exchange(sub).wait_send()
-        rs_first(sub).wait_send()
-        rs_second(sub).wait_send()
-        for k in range(1, zs):
-            rs_third(sub, k).wait_send()
+        for f in range(cuts):
+            part_exchange(sub, f).wait_send()
+        for p in range(pieces):
+            rs_first(sub, p).wait_send()
+            rs_second(sub, p).wait_send()
+            for k in range(1, zs):
+                rs_third(sub, p, k).wait_send()
+
+
+def emit_kernel(ig, qd, od, qr, out_r, ig_ref, qd_ref, od_ref, qr_ref, or_ref):
+    ig_ref[...] = ig[...]
+    qd_ref[...] = qd[...]
+    od_ref[...] = od[...].T
+    qr_ref[...] = qr[...]
+    or_ref[...] = out_r[...].T
 
 
 def shards_by_head(
@@ -609,7 +670,9 @@
     tokens = rows * bins
     cols = qkv_range.shape[1]
     chunk = 2 * half // seq
-    width = cols + half
+    lanes = 128
+    cuts = half // lanes
+    pieces = cols // half + 1
     span = bins // seq
     dma = pltpu.SemaphoreType.DMA
     vmem = pl.BlockSpec(memory_space=pltpu.VMEM)
@@ -628,34 +691,34 @@
         pltpu.VMEM((tokens, cols), BF16),
         pltpu.VMEM((tokens, half), BF16),
         pltpu.VMEM((tokens, half), F32),
-        pltpu.VMEM((2, tokens, half), BF16),
-        pltpu.VMEM((2, tokens, half), BF16),
-        pltpu.VMEM((rows * seq, span, half), F32),
-        pltpu.VMEM((rows * seq, span, half), BF16),
-        pltpu.VMEM((rows, bins, half), BF16),
-        pltpu.VMEM((tokens, half), BF16),
-        pltpu.VMEM((2, 2, seq // 4, 2, chunk, width), BF16),
-        pltpu.VMEM((2, 2, seq // 4, chunk, width), BF16),
-        pltpu.VMEM((2, zs, 2, chunk, width), BF16),
-        pltpu.VMEM((2, zs, chunk, width), BF16),
-        pltpu.VMEM((2, zs, chunk, width), BF16),
-        pltpu.VMEM((2, zs - 1, chunk, width), BF16),
+        pltpu.VMEM((2, cuts, tokens, lanes), BF16),
+        pltpu.VMEM((2, cuts, tokens, lanes), BF16),
+        pltpu.VMEM((rows * seq, span, lanes), F32),
+        pltpu.VMEM((cuts, rows * seq, span, lanes), BF16),
+        pltpu.VMEM((cuts, rows, bins, lanes), BF16),
+        pltpu.VMEM((cuts, tokens, lanes), BF16),
+        pltpu.VMEM((2, pieces, 2, seq // 4, 2, chunk, half), BF16),
+        pltpu.VMEM((2, pieces, 2, seq // 4, chunk, half), BF16),
+        pltpu.VMEM((2, pieces, zs, 2, chunk, half), BF16),
+        pltpu.VMEM((2, pieces, zs, chunk, half), BF16),
+        pltpu.VMEM((2, pieces, zs, chunk, half), BF16),
+        pltpu.VMEM((2, pieces, zs - 1, chunk, half), BF16),
         dma((4,)),
-        dma((4,)),
+        dma((3 + cuts,)),
         dma((2, seq)),
         dma((2, seq)),
         dma((2, seq)),
         dma((2, seq)),
         dma((2,)),
-        dma((2, 2)),
-        dma((seq,)),
-        dma((seq,)),
-        dma((2,)),
-        dma((2, 4)),
-        dma((2, zs - 1)),
-        dma((2, zs - 1)),
+        dma((2, cuts, 2)),
+        dma((cuts, seq)),
+        dma((cuts, seq)),
+        dma((cuts, 2)),
+        dma((2, pieces, 4)),
+        dma((2, pieces, zs - 1)),
+        dma((2, pieces, zs - 1)),
     ]
-    ig, qd, od, qr, out_r = pl.pallas_call(
+    results = pl.pallas_call(
         functools.partial(layer_kernel, seq),
         out_shape=(
             jax.ShapeDtypeStruct((tokens, half), BF16),
@@ -680,7 +743,20 @@
         qkv_range,
         out_range,
     )
-    return (ig.reshape(layer_cot.shape), qd, od.T, qr, out_r.T)
+    ig, qd, od, qr, out_r = pl.pallas_call(
+        emit_kernel,
+        out_shape=(
+            jax.ShapeDtypeStruct((tokens, half), BF16),
+            jax.ShapeDtypeStruct((chunk, cols), F32),
+            jax.ShapeDtypeStruct((half, chunk), F32),
+            jax.ShapeDtypeStruct((chunk, cols), F32),
+            jax.ShapeDtypeStruct((half, chunk), F32),
+        ),
+        in_specs=[vmem] * 5,
+        out_specs=(vmem,) * 5,
+        name="write_results",
+    )(*results)
+    return (ig.reshape(layer_cot.shape), qd, od, qr, out_r)
 
 
 def by_head(mesh):

time: 133 us -> 115 us (0.86)
  Pallas kernels: 124 us -> 110 us
  local copies, waits for them, and re-layouts: 7.24 us -> 3.34 us
    pallas_call x1, Pallas kernels: 124 us -> 108 us  [shards_by_head(): pl.pallas_call(functools.partial(layer_kernel, seq), out_shape=(jax.Shape...]
    unnamed x7 -> x2, local copies, waits for them, and re-layouts: 7.24 us -> 3.34 us
    pallas_call x0 -> x1, Pallas kernels: none -> 2.38 us  [shards_by_head(): pl.pallas_call(emit_kernel, out_shape=(jax.ShapeDtypeStruct((tokens, half...]
where the time goes in v3:
time: 115 us; the launch traced here: 114 us
  Pallas kernels  110 us (96%)
  local copies, waits for them, and re-layouts  3.34 us (3%)
    pallas_call x1, Pallas kernels, shards_by_head(): pl.pallas_call(functools.partial(layer_kernel, seq), out_shape=(jax.Shape...  108 us
    unnamed x2, local copies, waits for them, and re-layouts  3.34 us
    pallas_call x1, Pallas kernels, shards_by_head(): pl.pallas_call(emit_kernel, out_shape=(jax.ShapeDtypeStruct((tokens, half...  2.38 us

profile of v3, /device:TPU:0, one launch (start us, length us, event | category | flops | bytes accessed | tf_op | source)
XLA Modules:
  0.0 114.4 jit_solution(7746188346361179921)
XLA Ops:
  0.6 108.0 %axial_backward.1 = (bf16[512,384]{1,0:T(8,128)(2,1)}, f32[48,1152]{1,0:T(8,128)}, f32[48,384]{1,0:T(8,128)}, f32[48,1152]{1,0:T(8,128)}, f32[48,384]{1,0:T(8,128)}) custom-call(bf16[512,384]{1,0:T(8,128)(2,1)} %bitcast.2, bf16[2,256,384]{2,1,0:T(8,128)(2,1)} %rng_ref.1, bf16[2,256,384]{2,1,0:T(8,128)(2,1)} %cot_ref.1, bf16[768,1152]{1,0:T(8,128)(2,1)} %wqd_hbm.1, ...), custom_call_target="tpu_custom_call" | custom-call | tf_op jit(solution)/shard_map/axial_backward/pallas_call | solution.py:721
  108.7 2.4 %write_results.1 = (bf16[512,384]{1,0:T(8,128)(2,1)}, f32[48,1152]{1,0:T(8,128)}, f32[384,48]{1,0:T(8,128)}, f32[48,1152]{1,0:T(8,128)}, f32[384,48]{1,0:T(8,128)}) custom-call(bf16[512,384]{1,0:T(8,128)(2,1)} %get-tuple-element.15.ig, f32[48,1152]{1,0:T(8,128)} %get-tuple-element.16.qd, f32[48,384]{1,0:T(8,128)} %get-tuple-element.17.od, ...), custom_call_target="tpu_custom_call" | custom-call | tf_op jit(solution)/shard_map/write_results/pallas_call | solution.py:746
  111.0 1.7 %copy.12 = f32[384,48]{0,1:T(8,128)} copy(f32[384,48]{1,0:T(8,128)} %get-tuple-element.27) | data formatting | bytes 147456
  112.7 1.7 %copy.13 = f32[384,48]{0,1:T(8,128)} copy(f32[384,48]{1,0:T(8,128)} %get-tuple-element.29) | data formatting | bytes 147456

commit v4 on v3

--- a/solution.py
+++ b/solution.py
@@ -276,6 +276,15 @@
     cuts = half // lanes
     pieces = tiles + 1
 
+    core = lax.rem(s, 2)
+    xbit = lax.rem(s // 2, 2)
+    z = s // 4
+    zs = seq // 4
+    low = lax.rem(s, 4)
+
+    def peer_of(k):
+        return lax.rem(z + k // 4, zs) * 4 + lax.rem(low + lax.rem(k, 4), 4)
+
     def at_seq(q):
         return {"seq": q, "head": h}
 
@@ -303,7 +312,7 @@
     @pl.loop(1, seq)
     def _(k):
         pl.semaphore_signal(
-            barrier, inc=1, device_id=(lax.rem(s + k, seq), h), device_id_type=MESH
+            barrier, inc=1, device_id=(peer_of(k), h), device_id_type=MESH
         )
 
     pl.semaphore_signal(barrier, inc=1, device_id=(s, o), device_id_type=MESH)
@@ -312,7 +321,7 @@
     sources = (rng_ref, cot_ref)
 
     def exchange(a, k):
-        peer = lax.rem(s + k, seq)
+        peer = peer_of(k)
         return remote(
             sources[a].at[:, pl.ds(pl.multiple_of(peer * span, span), span), :],
             xr.at[a, h, pl.ds(s * rows, rows)],
@@ -322,7 +331,7 @@
         )
 
     def forward(a, k):
-        origin = lax.rem(s - k + seq, seq)
+        origin = lax.rem(z - k // 4 + zs, zs) * 4 + lax.rem(low - lax.rem(k, 4) + 4, 4)
         place = xr.at[a, h, pl.ds(origin * rows, rows)]
         return remote(place, place, fwd_s.at[a, k], fwd_r.at[a, k], pair)
 
@@ -341,16 +350,15 @@
         own.wait()
         forward(a, 0).start()
 
-    @pl.loop(1, seq)
-    def _(k):
-        for a in range(2):
-            exchange(a, k).wait_recv()
-            forward(a, k).start()
-
-    dop_send = remote(dop_ref, xs.at[1, 0, h], dx_sem.at[0], dx_sem.at[1], pair)
-    dop_send.start()
     dop_own = pltpu.make_async_copy(dop_ref, xs.at[1, 0, h], lsem.at[2])
     dop_own.start()
+
+    def forward_arrived(first, last):
+        @pl.loop(first, last)
+        def _(k):
+            for a in range(2):
+                exchange(a, k).wait_recv()
+                forward(a, k).start()
 
     def to_blocks(side):
         for a in range(2):
@@ -370,9 +378,9 @@
             at = pl.ds(pl.multiple_of(t * half, half), half)
             term = mm(xs[sub, 0, side], wq[sub, pl.ds(pl.multiple_of(side * half, half), half), at])
             if first:
-                pj32[:, at] = term
+                pj32[sub, :, at] = term
             else:
-                pj[:, at] = (pj32[:, at] + term).astype(BF16)
+                pj[:, at] = (pj32[sub, :, at] + term).astype(BF16)
 
     def project_cot(sub, side, first):
         at = pl.ds(pl.multiple_of(side * half, half), half)
@@ -402,6 +410,10 @@
         at = pl.ds(pl.multiple_of(side * half + f * lanes, lanes), lanes)
         return mm(gp[...], wq[sub, at, :], TAIL_CONTRACT)
 
+    def part_whole(sub, side):
+        at = pl.ds(pl.multiple_of(side * half, half), half)
+        return mm(gp[...], wq[sub, at, :], TAIL_CONTRACT)
+
     def part_exchange(sub, f):
         return remote(
             psend.at[sub, f],
@@ -419,10 +431,6 @@
     def cut(f):
         return slice(f * lanes, (f + 1) * lanes)
 
-    core = lax.rem(s, 2)
-    xbit = lax.rem(s // 2, 2)
-    z = s // 4
-    zs = seq // 4
     chunk = 2 * half // seq
 
     def grads(sub, p):
@@ -489,8 +497,15 @@
         else:
             q_out[:, p * half : (p + 1) * half] = total
 
-    loads[0].wait()
-    loads[1].wait()
+    forward_arrived(1, 4)
+    for load in loads:
+        load.wait()
+    dop_own.wait()
+    project(1, h, True)
+    turn(1, 0, h)
+    forward_arrived(4, seq)
+    dop_send = remote(dop_ref, xs.at[1, 0, h], dx_sem.at[0], dx_sem.at[1], pair)
+    dop_send.start()
     to_blocks(h)
     project(0, h, True)
     project_cot(0, h, True)
@@ -515,13 +530,12 @@
         attention(t, seq_mask)
 
     send_parts(0)
-    for f in range(cuts):
-        keep[:, cut(f)] = part_of(0, h, f)
+    keep[...] = part_whole(0, h)
     turn(0, 0, o)
     turn(0, 1, o)
 
     def give_back(f, k):
-        peer = lax.rem(s + k, seq)
+        peer = peer_of(k)
         return remote(
             rb.at[f, pl.ds(peer * rows, rows)],
             back.at[f, :, pl.ds(pl.multiple_of(s * span, span), span), :],
@@ -552,6 +566,10 @@
         )
         back_own[f].start()
         grads(0, f)
+        rs_first(0, f).start()
+
+    grads(0, tiles)
+    rs_first(0, tiles).start()
 
     def send_mid(f):
         return remote(
@@ -571,28 +589,21 @@
             mid[f, here, :] = new
             xs[1, 1, h, here, cut(f)] = new
         send_mid(f).start()
-
-    for p in range(cuts, pieces):
-        grads(0, p)
-    for p in range(pieces):
-        rs_first(0, p).start()
-    loads[2].wait()
-    loads[3].wait()
-    dop_own.wait()
-    project(1, h, True)
+        rs_after_first(0, f)
+
     project_cot(1, h, True)
-    for p in range(pieces):
-        rs_after_first(0, p)
+    rs_after_first(0, tiles)
     dop_send.wait_recv()
     project(1, o, False)
-    for side in range(2):
-        turn(1, 0, side)
+    for p in range(cuts):
+        rs_after_second(0, p)
+    turn(1, 0, o)
     turn(1, 1, h)
     for f in range(cuts):
         send_mid(f).wait_recv()
     project_cot(1, o, False)
-    for p in range(pieces):
-        rs_after_second(0, p)
+    turn(1, 1, o)
+    rs_after_second(0, tiles)
 
     @pl.loop(0, tiles)
     def _(t):
@@ -608,20 +619,18 @@
         def _():
             rs_after_second(1, t - 2)
 
-    send_parts(1)
-    rs_after_first(1, tiles - 1)
-    turn(1, 1, o)
     grads(1, tiles)
     rs_first(1, tiles).start()
-    for f in range(cuts):
-        keep[:, cut(f)] = part_of(1, h, f)
+    rs_after_first(1, tiles - 1)
+    send_parts(1)
+    rs_after_first(1, tiles)
     for p in range(max(tiles - 2, 0), tiles - 1):
         rs_after_second(1, p)
-    rs_after_first(1, tiles)
+    keep[...] = part_whole(1, h)
+    rs_after_second(1, tiles - 1)
     for p in range(pieces):
         rs_finish(0, p, qr_ref, or_ref)
-    for p in range(tiles - 1, pieces):
-        rs_after_second(1, p)
+    rs_after_second(1, tiles)
     for f in range(cuts):
         part_exchange(1, f).wait_recv()
         added = (keep[:, cut(f)] + precv[1, f].astype(F32)).astype(BF16).astype(F32)
@@ -657,9 +666,9 @@
 def emit_kernel(ig, qd, od, qr, out_r, ig_ref, qd_ref, od_ref, qr_ref, or_ref):
     ig_ref[...] = ig[...]
     qd_ref[...] = qd[...]
-    od_ref[...] = od[...].T
+    od_ref[...] = od[...]
     qr_ref[...] = qr[...]
-    or_ref[...] = out_r[...].T
+    or_ref[...] = out_r[...]
 
 
 def shards_by_head(
@@ -684,7 +693,7 @@
         pltpu.VMEM((2, 2, rows * seq, span, half), BF16),
         pltpu.VMEM((2, 2, 2, tokens, half), BF16),
         pltpu.VMEM((2, 2, 2, half, tokens), BF16),
-        pltpu.VMEM((tokens, cols), F32),
+        pltpu.VMEM((2, tokens, cols), F32),
         pltpu.VMEM((tokens, half), F32),
         pltpu.VMEM((tokens, cols), BF16),
         pltpu.VMEM((tokens, half), BF16),
@@ -748,15 +757,15 @@
         out_shape=(
             jax.ShapeDtypeStruct((tokens, half), BF16),
             jax.ShapeDtypeStruct((chunk, cols), F32),
-            jax.ShapeDtypeStruct((half, chunk), F32),
+            jax.ShapeDtypeStruct((chunk, half), F32),
             jax.ShapeDtypeStruct((chunk, cols), F32),
-            jax.ShapeDtypeStruct((half, chunk), F32),
+            jax.ShapeDtypeStruct((chunk, half), F32),
         ),
         in_specs=[vmem] * 5,
         out_specs=(vmem,) * 5,
         name="write_results",
     )(*results)
-    return (ig.reshape(layer_cot.shape), qd, od, qr, out_r)
+    return (ig.reshape(layer_cot.shape), qd, od.T, qr, out_r.T)
 
 
 def by_head(mesh):

time: 115 us -> 104 us (0.904)
  Pallas kernels: 110 us -> 103 us
  local copies, waits for them, and re-layouts: 3.34 us -> 0 us
    pallas_call x1, Pallas kernels: 108 us -> 101 us  [shards_by_head(): pl.pallas_call(functools.partial(layer_kernel, seq), out_shape=(jax.Shape...]
    unnamed x2 -> x0, local copies, waits for them, and re-layouts: 3.34 us -> none
where the time goes in v4:
time: 104 us; the launch traced here: 103 us
  Pallas kernels  103 us (99%)
    pallas_call x1, Pallas kernels, shards_by_head(): pl.pallas_call(functools.partial(layer_kernel, seq), out_shape=(jax.Shape...  101 us
    pallas_call x1, Pallas kernels, shards_by_head(): pl.pallas_call(emit_kernel, out_shape=(jax.ShapeDtypeStruct((tokens, half...  2.2 us

profile of v4, /device:TPU:0, one launch (start us, length us, event | category | flops | bytes accessed | tf_op | source)
XLA Modules:
  0.0 103.4 jit_solution(9579200214164418714)
XLA Ops:
  0.6 100.6 %axial_backward.1 = (bf16[512,384]{1,0:T(8,128)(2,1)}, f32[48,1152]{1,0:T(8,128)}, f32[48,384]{1,0:T(8,128)}, f32[48,1152]{1,0:T(8,128)}, f32[48,384]{1,0:T(8,128)}) custom-call(bf16[512,384]{1,0:T(8,128)(2,1)} %bitcast.4, bf16[2,256,384]{2,1,0:T(8,128)(2,1)} %rng_ref.1, bf16[2,256,384]{2,1,0:T(8,128)(2,1)} %cot_ref.1, bf16[768,1152]{1,0:T(8,128)(2,1)} %wqd_hbm.1, ...), custom_call_target="tpu_custom_call" | custom-call | tf_op jit(solution)/shard_map/axial_backward/pallas_call | solution.py:730
  101.2 2.2 %write_results.1 = (bf16[512,384]{1,0:T(8,128)(2,1)}, f32[48,1152]{1,0:T(8,128)}, f32[48,384]{1,0:T(8,128)}, f32[48,1152]{1,0:T(8,128)}, f32[48,384]{1,0:T(8,128)}) custom-call(bf16[512,384]{1,0:T(8,128)(2,1)} %get-tuple-element.15.ig, f32[48,1152]{1,0:T(8,128)} %get-tuple-element.16.qd, f32[48,384]{1,0:T(8,128)} %get-tuple-element.17.od, ...), custom_call_target="tpu_custom_call" | custom-call | tf_op jit(solution)/shard_map/write_results/pallas_call | solution.py:755
